TPU v7x, 256 devices: a whole 4x4x8 slice. The times are simulated.
256 devices in a mesh: row: 32 (over y, z), col: 8 (over x, core).
Axes of the slice: x: 4, y: 4, z: 8, core: 2. Of those that a mesh axis runs over, the one named last changes fastest.
Arguments:
- hessian: bfloat16 [8, 3328, 26624], P(None, 'row', 'col'), may hold values from -0.026001572 to 5, as said below
- exponents: int32 [26624], P(('col', 'row')), may hold values from 0 to 1
- masks: int32 [26624, 256], P(('col', 'row')), may hold values 0 or 1
- weights: bfloat16 [26624, 256], P(('col', 'row')), may hold values from -12 to 12
Outputs:
- solution_field: float32 [26624, 256], P(('col', 'row'))
- residual: float32 [26624, 256], P(('col', 'row'))
Inputs may be any that keep to these rules, and one draw needn't show every extreme that they name: `hessian`: read as an 26624 x 26624 matrix it is symmetric and positive definite.
All inputs are finite; a program needn't handle non-finite values. No bound on the sum of `masks` on one device may be relied on, other than what follows from the above.
Results may differ from a plain program's by a relative error of at most 0.014.
Values may be sent and summed in bfloat16 or wider, within the bound.
No kernel may reach another device: no remote copies, remote signals or barrier semaphores. Data moves between devices by JAX's collectives and lax.ppermute only.
A program may use at most 64 MiB of HBM per device.

v0:
```python
import jax
import jax.numpy as jnp
from jax import lax
from jax.sharding import Mesh, PartitionSpec as P

Y, ZS, ZP, X, CORE = 4, 4, 2, 4, 2
BF16, F32 = jnp.bfloat16, jnp.float32
ROUNDING, ALLOWED = 8e-4, 8.5e-3


def spread(block, axes, size):
    return lax.all_to_all(jnp.broadcast_to(block[None], (size,) + block.shape), axes, 0, 0, tiled=True)


def moved(block, axis, size, shift):
    return lax.ppermute(block, axis, [(i, (i + shift) % size) for i in range(size)])


def around(block, axis, size):
    place = lax.axis_index(axis)
    whole = jnp.zeros((size,) + block.shape, block.dtype)
    whole = lax.dynamic_update_index_in_dim(whole, block, place, 0)
    for shift in (2, 1, 3):
        whole = lax.dynamic_update_index_in_dim(whole, moved(block, axis, size, shift), (place + size - shift) % size, 0)
    return whole


def gather_rows(block):
    place, pair = lax.axis_index("y"), lax.axis_index("zp")
    swap = [(0, 1), (1, 0)]
    strided = around(block, "zs", ZS)
    mine = {shift: moved(strided, "y", Y, shift) for shift in (2, 1, 3)}
    paired = lax.ppermute(strided, "zp", swap)
    other = {shift: moved(paired, "y", Y, shift) for shift in (1, 3)}
    other[2] = lax.ppermute(mine[2], "zp", swap)
    mine[0], other[0] = strided, paired
    whole = jnp.zeros((Y, ZS, ZP) + block.shape, block.dtype)
    for pieces, half in ((mine, pair), (other, 1 - pair)):
        for shift, piece in pieces.items():
            at = ((place + Y - shift) % Y, 0, half, 0, 0)
            whole = lax.dynamic_update_slice(whole, piece[None, :, None], at)
    return whole.reshape((Y * ZS * ZP,) + block.shape)


def scatter_rows(partial_sum):
    core = lax.axis_index("core")
    place = lax.axis_index("x")
    split = partial_sum.reshape((X, CORE) + partial_sum.shape[1:])
    mine = lax.dynamic_index_in_dim(split, core, 1, keepdims=False)
    other = lax.dynamic_index_in_dim(split, 1 - core, 1, keepdims=False)
    half = mine + lax.ppermute(other, "core", [(0, 1), (1, 0)])
    total = lax.dynamic_index_in_dim(half, place, 0, keepdims=False)
    for shift in (2, 1, 3):
        total = total + moved(lax.dynamic_index_in_dim(half, (place + shift) % X, 0, keepdims=False), "x", X, shift)
    return total


def gather_rows_seldom(block):
    strided = spread(block, "zs", ZS)
    whole = spread(strided, ("y", "zp"), Y * ZP)
    whole = whole.reshape((Y, ZP, ZS) + block.shape).transpose(0, 2, 1, 3, 4)
    return whole.reshape((Y * ZS * ZP,) + block.shape)


def scatter_rows_seldom(partial_sum):
    return jnp.sum(lax.all_to_all(partial_sum, ("x", "core"), 0, 0, tiled=True), axis=0)


def total_sums(rows):
    sums = jnp.stack([jnp.sum(first * second, axis=0) for first, second in rows])
    sums = jnp.pad(sums, ((0, 8 - len(rows)), (0, 0)))
    sums = jnp.sum(spread(sums, ("x", "core"), X * CORE), axis=0)
    return jnp.sum(spread(sums, ("y", "zs", "zp"), Y * ZS * ZP), axis=0)


def on_device(hessian, exponents, masks, weights):
    row_scale = jnp.exp2(-exponents.astype(F32))[:, None]
    kept = masks.astype(F32)
    dense = weights.astype(F32)
    rows = exponents.shape[0]

    def product(gathered):
        gathered = gathered.reshape(-1, gathered.shape[-1])
        return jnp.einsum("cst,tk->csk", hessian, gathered, preferred_element_type=F32)

    gain = kept * row_scale
    start = lax.axis_index(("y", "zs", "zp")) * rows
    block = lax.axis_index(("x", "core"))

    def turn(index, state):
        payload, found, last_partial, last_shift = state
        last = lax.dynamic_index_in_dim(found, jnp.maximum(index - 1, 0), 0, keepdims=False)

        gathered = gather_rows(payload)
        tails = jnp.sum(gathered[:, rows : rows + 2].astype(F32), axis=0)
        shift = jnp.where(tails[1] > 0.0, tails[0] / tails[1], last_shift)
        partial_sum = product(gathered[:, :rows]) + last_shift * last_partial
        vectors = gain * scatter_rows(partial_sum)

        own_rows = lax.dynamic_index_in_dim(hessian, block + jnp.minimum(index, 0), 0, keepdims=False)
        on_diagonal = lax.broadcasted_iota(jnp.int32, own_rows.shape, 1) == start + lax.broadcasted_iota(
            jnp.int32, own_rows.shape, 0
        )
        diagonal = jnp.sum(jnp.where(on_diagonal, own_rows.astype(F32), 0.0), axis=1, keepdims=True)

        scaled = row_scale * vectors
        tail = jnp.stack([jnp.sum(diagonal * scaled * scaled, axis=0), jnp.sum(vectors * vectors, axis=0)])
        tail = jnp.pad(jnp.where(index == 0, tail, 0.0), ((0, 6), (0, 0)))
        payload = jnp.concatenate([scaled - shift * (row_scale * last), tail]).astype(BF16)
        found = lax.dynamic_update_index_in_dim(found, vectors, index, 0)
        return payload, found, partial_sum, shift

    payload = jnp.pad((row_scale * ((1.0 - kept) * dense)).astype(BF16), ((0, 8), (0, 0)))
    found = jnp.zeros((3,) + dense.shape, F32)
    partial_sum = jnp.zeros(hessian.shape[:2] + dense.shape[1:], F32)
    _, (v0, v1, v2), _, shift = lax.fori_loop(0, 3, turn, (payload, found, partial_sum, partial_sum[0, 0]))

    g00, g01, g11, g02, g12, g22, h1, h2 = total_sums(
        [(v0, v0), (v0, v1), (v1, v1), (v0, v2), (v1, v2), (v2, v2), (v0, shift * v0), (shift * v0, shift * v0)]
    )
    step_0 = g00 / g01
    residual = v0 - step_0 * v1
    fresh = g00 - 2.0 * step_0 * g01 + step_0 * step_0 * g11
    ahead = 1.0 + fresh / g00
    along = ahead * ahead * g01 - ahead * step_0 * (g02 + g11) + step_0 * step_0 * g12
    step_1 = fresh / along

    direction_sq = ahead * ahead * g00 - 2.0 * ahead * step_0 * g01 + step_0 * step_0 * g11
    left_sq = ahead * ahead * g00 - 2.0 * ahead * step_0 * h1 + step_0 * step_0 * h2
    with_image = ahead * g01 - step_0 * (g02 + ahead * g11) + step_0 * step_0 * g12
    image_sq = ahead * ahead * g11 - 2.0 * ahead * step_0 * g12 + step_0 * step_0 * g22
    last_sq = fresh - 2.0 * step_1 * with_image + step_1 * step_1 * image_sq
    spread_sq = left_sq + direction_sq + (jnp.sqrt(left_sq) + jnp.sqrt(direction_sq)) ** 2
    error_sq = ROUNDING**2 * jnp.sum(step_1 * step_1 * (g11 / g00) * spread_sq)
    close = error_sq < ALLOWED**2 * jnp.sum(last_sq)

    def short():
        direction = ahead * v0 - step_0 * v1
        image = ahead * v1 - step_0 * v2
        return (kept * dense + step_0 * v0 + step_1 * direction, residual - step_1 * image)

    def long():
        fresh = total_sums([(residual, residual)])[0]
        direction = residual + fresh / g00 * v0
        partial_sum = product(gather_rows_seldom((row_scale * direction).astype(BF16)))
        image = kept * row_scale * scatter_rows_seldom(partial_sum)
        step = fresh / total_sums([(direction, image)])[0]
        return (kept * dense + step_0 * v0 + step * direction, residual - step * image)

    return lax.cond(close, short, long)


def solution(mesh):
    fine = Mesh(mesh.devices.reshape(Y, ZS, ZP, X, CORE), ("y", "zs", "zp", "x", "core"))
    row = ("y", "zs", "zp")
    owner = ("x", "core") + row
    in_specs = (P(None, row, ("x", "core")), P(owner), P(owner, None), P(owner, None))
    out_specs = (P(owner, None), P(owner, None))
    return jax.shard_map(on_device, mesh=fine, in_specs=in_specs, out_specs=out_specs, check_vma=False)
```

profile of v0, /device:TPU:32, one launch (start us, length us, event | category | flops | bytes accessed | tf_op | source)
XLA Modules:
  0.0 169.0 jit_solution(5154153711113643352)
XLA Ops:
  2.4 135.9 %while.25 = (s32[]{:T(128)}, bf16[112,256]{1,0:T(8,128)(2,1)S(1)}, f32[3,104,256]{2,1,0:T(8,128)S(1)}, f32[8,104,256]{2,1,0:T(8,128)S(1)}, f32[256]{0:T(256)S(1)...) while((s32[]{:T(128)}, bf16[112,256]{1,0:T(8,128)(2,1)S(1)}, ...), condition=%wide.region_5.6_spmd.clone, body=%wide.region_0.5_spmd.clone.sunk | while | flops 1420384896 | bytes 56708472 | solution.py:116
  2.4 6.4 %collective-permute-start = (bf16[112,256]{1,0:T(8,128)(2,1)S(1)}, bf16[112,256]{1,0:T(8,128)(2,1)S(1)}, u32[]{:S(2)}, u32[]{:S(2)}) collective-permute-start(bf16[112,256]{1,0:T(8,128)(2,1)S(1)} %get-tuple-element.652), channel_id=1, source_target_pairs={{0,32},{16,48},{32,0},{48,16},{1,33},{17,49},{33,1},{49,17},{2,34}... | collective-permute-start | bytes 172040 | tf_op jit(solution)/shard_map/while/body/eval_jaxpr/ppermute | solution.py:16
  10.2 2.7 %collective-permute-start.2 = (bf16[112,256]{1,0:T(8,128)(2,1)S(1)}, bf16[112,256]{1,0:T(8,128)(2,1)S(1)}, u32[]{:S(2)}, u32[]{:S(2)}) collective-permute-start(bf16[112,256]{1,0:T(8,128)(2,1)S(1)} %get-tuple-element.652), channel_id=1, source_target_pairs={{0,48},{16,0},{32,16},{48,32},{1,49},{17,1},{33,17},{49,33},{2,50}... | collective-permute-start | bytes 172040 | tf_op jit(solution)/shard_map/while/body/eval_jaxpr/ppermute | solution.py:16
  13.0 3.0 %collective-permute-done.1 = bf16[112,256]{1,0:T(8,128)(2,1)S(1)} collective-permute-done((bf16[112,256]{1,0:T(8,128)(2,1)S(1)}, bf16[112,256]{1,0:T(8,128)(2,1)S(1)}, u32[]{:S(2)}, u32[]{:S(2)}) %collective-permute-start.1) | collective-permute-done | bytes 57376 | tf_op jit(solution)/shard_map/while/body/eval_jaxpr/ppermute | solution.py:16
  16.6 3.2 %collective-permute-start.3 = (bf16[4,112,256]{2,1,0:T(8,128)(2,1)S(1)}, bf16[4,112,256]{2,1,0:T(8,128)(2,1)S(1)}, u32[]{:S(2)}, u32[]{:S(2)}) collective-permute-start(bf16[4,112,256]{2,1,0:T(8,128)(2,1)S(1)} %bitcast_dynamic-update-slice_fusion.29), channel_id=1, source_target_pairs={{0,128},{64,192},{128,0},{192,64},{1,129},{65,193},{129,1},{193,65... | collective-permute-start | bytes 688136 | tf_op jit(solution)/shard_map/while/body/eval_jaxpr/ppermute | solution.py:16
  20.5 2.6 %collective-permute-start.5 = (bf16[4,112,256]{2,1,0:T(8,128)(2,1)S(1)}, bf16[4,112,256]{2,1,0:T(8,128)(2,1)S(1)}, u32[]{:S(2)}, u32[]{:S(2)}) collective-permute-start(bf16[4,112,256]{2,1,0:T(8,128)(2,1)S(1)} %bitcast_dynamic-update-slice_fusion.29), channel_id=1, source_target_pairs={{0,192},{64,0},{128,64},{192,128},{1,193},{65,1},{129,65},{193,129... | collective-permute-start | bytes 688136 | tf_op jit(solution)/shard_map/while/body/eval_jaxpr/ppermute | solution.py:16
  23.6 2.7 %collective-permute-start.8 = (bf16[4,112,256]{2,1,0:T(8,128)(2,1)S(1)}, bf16[4,112,256]{2,1,0:T(8,128)(2,1)S(1)}, u32[]{:S(2)}, u32[]{:S(2)}) collective-permute-start(bf16[4,112,256]{2,1,0:T(8,128)(2,1)S(1)} %collective-permute-done.6), channel_id=1, source_target_pairs={{0,192},{64,0},{128,64},{192,128},{1,193},{65,1},{129,65},{193,129... | collective-permute-start | bytes 688136 | tf_op jit(solution)/shard_map/while/body/eval_jaxpr/ppermute | solution.py:16
  38.5 2.8 %collective-permute-start.11 = (f32[104,256]{1,0:T(8,128)S(1)}, f32[104,256]{1,0:T(8,128)S(1)}, u32[]{:S(2)}, u32[]{:S(2)}) collective-permute-start(f32[104,256]{1,0:T(8,128)S(1)} %get-tuple-element.620), channel_id=1, source_target_pairs={{0,6},{2,0},{4,2},{6,4},{1,7},{3,1},{5,3},{7,5},{8,14},{10,8},{12,... | collective-permute-start | bytes 319496 | tf_op jit(solution)/shard_map/while/body/eval_jaxpr/ppermute | solution.py:16
  45.1 4.4 %collective-permute-done.12 = f32[104,256]{1,0:T(8,128)S(1)} collective-permute-done((f32[104,256]{1,0:T(8,128)S(1)}, f32[104,256]{1,0:T(8,128)S(1)}, u32[]{:S(2)}, u32[]{:S(2)}) %collective-permute-start.12) | collective-permute-done | bytes 106528 | tf_op jit(solution)/shard_map/while/body/eval_jaxpr/ppermute | solution.py:16
  49.7 4.8 %collective-permute-start = (bf16[112,256]{1,0:T(8,128)(2,1)S(1)}, bf16[112,256]{1,0:T(8,128)(2,1)S(1)}, u32[]{:S(2)}, u32[]{:S(2)}) collective-permute-start(bf16[112,256]{1,0:T(8,128)(2,1)S(1)} %get-tuple-element.652), channel_id=1, source_target_pairs={{0,32},{16,48},{32,0},{48,16},{1,33},{17,49},{33,1},{49,17},{2,34}... | collective-permute-start | bytes 172040 | tf_op jit(solution)/shard_map/while/body/eval_jaxpr/ppermute | solution.py:16
  56.1 2.5 %collective-permute-start.2 = (bf16[112,256]{1,0:T(8,128)(2,1)S(1)}, bf16[112,256]{1,0:T(8,128)(2,1)S(1)}, u32[]{:S(2)}, u32[]{:S(2)}) collective-permute-start(bf16[112,256]{1,0:T(8,128)(2,1)S(1)} %get-tuple-element.652), channel_id=1, source_target_pairs={{0,48},{16,0},{32,16},{48,32},{1,49},{17,1},{33,17},{49,33},{2,50}... | collective-permute-start | bytes 172040 | tf_op jit(solution)/shard_map/while/body/eval_jaxpr/ppermute | solution.py:16
  58.7 2.8 %collective-permute-done.1 = bf16[112,256]{1,0:T(8,128)(2,1)S(1)} collective-permute-done((bf16[112,256]{1,0:T(8,128)(2,1)S(1)}, bf16[112,256]{1,0:T(8,128)(2,1)S(1)}, u32[]{:S(2)}, u32[]{:S(2)}) %collective-permute-start.1) | collective-permute-done | bytes 57376 | tf_op jit(solution)/shard_map/while/body/eval_jaxpr/ppermute | solution.py:16
  77.1 3.1 %collective-permute-done.7 = bf16[4,112,256]{2,1,0:T(8,128)(2,1)S(1)} collective-permute-done((bf16[4,112,256]{2,1,0:T(8,128)(2,1)S(1)}, bf16[4,112,256]{2,1,0:T(8,128)(2,1)S(1)}, u32[]{:S(2)}, u32[]{:S(2)}) %collective-permute-start.7) | collective-permute-done | bytes 229408 | tf_op jit(solution)/shard_map/while/body/eval_jaxpr/ppermute | solution.py:16
  90.1 3.2 %collective-permute-done.12 = f32[104,256]{1,0:T(8,128)S(1)} collective-permute-done((f32[104,256]{1,0:T(8,128)S(1)}, f32[104,256]{1,0:T(8,128)S(1)}, u32[]{:S(2)}, u32[]{:S(2)}) %collective-permute-start.12) | collective-permute-done | bytes 106528 | tf_op jit(solution)/shard_map/while/body/eval_jaxpr/ppermute | solution.py:16
  93.5 3.5 %collective-permute-start = (bf16[112,256]{1,0:T(8,128)(2,1)S(1)}, bf16[112,256]{1,0:T(8,128)(2,1)S(1)}, u32[]{:S(2)}, u32[]{:S(2)}) collective-permute-start(bf16[112,256]{1,0:T(8,128)(2,1)S(1)} %get-tuple-element.652), channel_id=1, source_target_pairs={{0,32},{16,48},{32,0},{48,16},{1,33},{17,49},{33,1},{49,17},{2,34}... | collective-permute-start | bytes 172040 | tf_op jit(solution)/shard_map/while/body/eval_jaxpr/ppermute | solution.py:16
  98.6 2.5 %collective-permute-start.2 = (bf16[112,256]{1,0:T(8,128)(2,1)S(1)}, bf16[112,256]{1,0:T(8,128)(2,1)S(1)}, u32[]{:S(2)}, u32[]{:S(2)}) collective-permute-start(bf16[112,256]{1,0:T(8,128)(2,1)S(1)} %get-tuple-element.652), channel_id=1, source_target_pairs={{0,48},{16,0},{32,16},{48,32},{1,49},{17,1},{33,17},{49,33},{2,50}... | collective-permute-start | bytes 172040 | tf_op jit(solution)/shard_map/while/body/eval_jaxpr/ppermute | solution.py:16
  108.6 2.6 %collective-permute-start.5 = (bf16[4,112,256]{2,1,0:T(8,128)(2,1)S(1)}, bf16[4,112,256]{2,1,0:T(8,128)(2,1)S(1)}, u32[]{:S(2)}, u32[]{:S(2)}) collective-permute-start(bf16[4,112,256]{2,1,0:T(8,128)(2,1)S(1)} %bitcast_dynamic-update-slice_fusion.29), channel_id=1, source_target_pairs={{0,192},{64,0},{128,64},{192,128},{1,193},{65,1},{129,65},{193,129... | collective-permute-start | bytes 688136 | tf_op jit(solution)/shard_map/while/body/eval_jaxpr/ppermute | solution.py:16
  111.6 2.9 %collective-permute-start.8 = (bf16[4,112,256]{2,1,0:T(8,128)(2,1)S(1)}, bf16[4,112,256]{2,1,0:T(8,128)(2,1)S(1)}, u32[]{:S(2)}, u32[]{:S(2)}) collective-permute-start(bf16[4,112,256]{2,1,0:T(8,128)(2,1)S(1)} %collective-permute-done.6), channel_id=1, source_target_pairs={{0,192},{64,0},{128,64},{192,128},{1,193},{65,1},{129,65},{193,129... | collective-permute-start | bytes 688136 | tf_op jit(solution)/shard_map/while/body/eval_jaxpr/ppermute | solution.py:16
  116.6 2.8 %collective-permute-done.4 = bf16[4,112,256]{2,1,0:T(8,128)(2,1)S(1)} collective-permute-done((bf16[4,112,256]{2,1,0:T(8,128)(2,1)S(1)}, bf16[4,112,256]{2,1,0:T(8,128)(2,1)S(1)}, u32[]{:S(2)}, u32[]{:S(2)}) %collective-permute-start.4) | collective-permute-done | bytes 229408 | tf_op jit(solution)/shard_map/while/body/eval_jaxpr/ppermute | solution.py:16
  126.5 3.2 %collective-permute-start.11 = (f32[104,256]{1,0:T(8,128)S(1)}, f32[104,256]{1,0:T(8,128)S(1)}, u32[]{:S(2)}, u32[]{:S(2)}) collective-permute-start(f32[104,256]{1,0:T(8,128)S(1)} %get-tuple-element.620), channel_id=1, source_target_pairs={{0,6},{2,0},{4,2},{6,4},{1,7},{3,1},{5,3},{7,5},{8,14},{10,8},{12,... | collective-permute-start | bytes 319496 | tf_op jit(solution)/shard_map/while/body/eval_jaxpr/ppermute | solution.py:16
  132.8 5.2 %collective-permute-done.12 = f32[104,256]{1,0:T(8,128)S(1)} collective-permute-done((f32[104,256]{1,0:T(8,128)S(1)}, f32[104,256]{1,0:T(8,128)S(1)}, u32[]{:S(2)}, u32[]{:S(2)}) %collective-permute-start.12) | collective-permute-done | bytes 106528 | tf_op jit(solution)/shard_map/while/body/eval_jaxpr/ppermute | solution.py:16
  138.5 8.0 %all_to_all.45 = f32[8,8,256]{2,1,0:T(8,128)S(1)} all-to-all(f32[8,8,256]{2,1,0:T(8,128)S(1)} %broadcast_in_dim.298), channel_id=1, replica_groups=mesh['y'=4,'zs'=4,'zp'=2,'x'=4,'core'=2] {'x','core'}, dimensions={0} | all-to-all | bytes 131072 | tf_op jit(solution)/shard_map/all_to_all | solution.py:12
  147.2 6.7 %all-to-all-start.8 = ((f32[32,8,256]{2,1,0:T(8,128)}), f32[32,8,256]{2,1,0:T(8,128)S(1)}, u32[]{:S(2)}, u32[]{:S(2)}) async-start(f32[32,8,256]{2,1,0:T(8,128)} %broadcast_in_dim.299), calls=%async_computation.8 | async-start | bytes 524288 | tf_op jit(solution)/shard_map/all_to_all | solution.py:12
  154.0 12.1 %all-to-all-done.8 = f32[32,8,256]{2,1,0:T(8,128)S(1)} async-done(((f32[32,8,256]{2,1,0:T(8,128)}), f32[32,8,256]{2,1,0:T(8,128)S(1)}, u32[]{:S(2)}, u32[]{:S(2)}) %all-to-all-start.8) | async-done | bytes 262176 | tf_op jit(solution)/shard_map/all_to_all | solution.py:12
  (192 shorter events, 72.1 us)
Async XLA Ops:
  2.4 10.6 %collective-permute-start = (bf16[112,256]{1,0:T(8,128)(2,1)S(1)}, bf16[112,256]{1,0:T(8,128)(2,1)S(1)}, u32[]{:S(2)}, u32[]{:S(2)}) collective-permute-start(bf16[112,256]{1,0:T(8,128)(2,1)S(1)} %get-tuple-element.652), channel_id=1, source_target_pairs={{0,32},{16,48},{32,0},{48,16},{1,33},{17,49},{33,1},{49,17},{2,34}... | collective-permute-start | bytes 172040 | tf_op jit(solution)/shard_map/while/body/eval_jaxpr/ppermute | solution.py:16
  16.6 10.0 %collective-permute-start.3 = (bf16[4,112,256]{2,1,0:T(8,128)(2,1)S(1)}, bf16[4,112,256]{2,1,0:T(8,128)(2,1)S(1)}, u32[]{:S(2)}, u32[]{:S(2)}) collective-permute-start(bf16[4,112,256]{2,1,0:T(8,128)(2,1)S(1)} %bitcast_dynamic-update-slice_fusion.29), channel_id=1, source_target_pairs={{0,128},{64,192},{128,0},{192,64},{1,129},{65,193},{129,1},{193,65... | collective-permute-start | bytes 688136 | tf_op jit(solution)/shard_map/while/body/eval_jaxpr/ppermute | solution.py:16
  19.8 10.8 %collective-permute-start.4 = (bf16[4,112,256]{2,1,0:T(8,128)(2,1)S(1)}, bf16[4,112,256]{2,1,0:T(8,128)(2,1)S(1)}, u32[]{:S(2)}, u32[]{:S(2)}) collective-permute-start(bf16[4,112,256]{2,1,0:T(8,128)(2,1)S(1)} %bitcast_dynamic-update-slice_fusion.29), channel_id=1, source_target_pairs={{0,64},{64,128},{128,192},{192,0},{1,65},{65,129},{129,193},{193,1... | collective-permute-start | bytes 688136 | tf_op jit(solution)/shard_map/while/body/eval_jaxpr/ppermute | solution.py:16
  20.5 11.2 %collective-permute-start.5 = (bf16[4,112,256]{2,1,0:T(8,128)(2,1)S(1)}, bf16[4,112,256]{2,1,0:T(8,128)(2,1)S(1)}, u32[]{:S(2)}, u32[]{:S(2)}) collective-permute-start(bf16[4,112,256]{2,1,0:T(8,128)(2,1)S(1)} %bitcast_dynamic-update-slice_fusion.29), channel_id=1, source_target_pairs={{0,192},{64,0},{128,64},{192,128},{1,193},{65,1},{129,65},{193,129... | collective-permute-start | bytes 688136 | tf_op jit(solution)/shard_map/while/body/eval_jaxpr/ppermute | solution.py:16
  23.1 10.9 %collective-permute-start.7 = (bf16[4,112,256]{2,1,0:T(8,128)(2,1)S(1)}, bf16[4,112,256]{2,1,0:T(8,128)(2,1)S(1)}, u32[]{:S(2)}, u32[]{:S(2)}) collective-permute-start(bf16[4,112,256]{2,1,0:T(8,128)(2,1)S(1)} %collective-permute-done.6), channel_id=1, source_target_pairs={{0,64},{64,128},{128,192},{192,0},{1,65},{65,129},{129,193},{193,1... | collective-permute-start | bytes 688136 | tf_op jit(solution)/shard_map/while/body/eval_jaxpr/ppermute | solution.py:16
  23.6 10.6 %collective-permute-start.8 = (bf16[4,112,256]{2,1,0:T(8,128)(2,1)S(1)}, bf16[4,112,256]{2,1,0:T(8,128)(2,1)S(1)}, u32[]{:S(2)}, u32[]{:S(2)}) collective-permute-start(bf16[4,112,256]{2,1,0:T(8,128)(2,1)S(1)} %collective-permute-done.6), channel_id=1, source_target_pairs={{0,192},{64,0},{128,64},{192,128},{1,193},{65,1},{129,65},{193,129... | collective-permute-start | bytes 688136 | tf_op jit(solution)/shard_map/while/body/eval_jaxpr/ppermute | solution.py:16
  41.3 8.2 %collective-permute-start.12 = (f32[104,256]{1,0:T(8,128)S(1)}, f32[104,256]{1,0:T(8,128)S(1)}, u32[]{:S(2)}, u32[]{:S(2)}) collective-permute-start(f32[104,256]{1,0:T(8,128)S(1)} %get-tuple-element.621), channel_id=1, source_target_pairs={{0,2},{2,4},{4,6},{6,0},{1,3},{3,5},{5,7},{7,1},{8,10},{10,12},{12... | collective-permute-start | bytes 319496 | tf_op jit(solution)/shard_map/while/body/eval_jaxpr/ppermute | solution.py:16
  41.3 8.2 %collective-permute-start.13 = (f32[104,256]{1,0:T(8,128)S(1)}, f32[104,256]{1,0:T(8,128)S(1)}, u32[]{:S(2)}, u32[]{:S(2)}) collective-permute-start(f32[104,256]{1,0:T(8,128)S(1)} %get-tuple-element.622), channel_id=1, source_target_pairs={{0,4},{2,6},{4,0},{6,2},{1,5},{3,7},{5,1},{7,3},{8,12},{10,14},{12... | collective-permute-start | bytes 319496 | tf_op jit(solution)/shard_map/while/body/eval_jaxpr/ppermute | solution.py:16
  49.7 9.0 %collective-permute-start = (bf16[112,256]{1,0:T(8,128)(2,1)S(1)}, bf16[112,256]{1,0:T(8,128)(2,1)S(1)}, u32[]{:S(2)}, u32[]{:S(2)}) collective-permute-start(bf16[112,256]{1,0:T(8,128)(2,1)S(1)} %get-tuple-element.652), channel_id=1, source_target_pairs={{0,32},{16,48},{32,0},{48,16},{1,33},{17,49},{33,1},{49,17},{2,34}... | collective-permute-start | bytes 172040 | tf_op jit(solution)/shard_map/while/body/eval_jaxpr/ppermute | solution.py:16
  62.0 10.1 %collective-permute-start.3 = (bf16[4,112,256]{2,1,0:T(8,128)(2,1)S(1)}, bf16[4,112,256]{2,1,0:T(8,128)(2,1)S(1)}, u32[]{:S(2)}, u32[]{:S(2)}) collective-permute-start(bf16[4,112,256]{2,1,0:T(8,128)(2,1)S(1)} %bitcast_dynamic-update-slice_fusion.29), channel_id=1, source_target_pairs={{0,128},{64,192},{128,0},{192,64},{1,129},{65,193},{129,1},{193,65... | collective-permute-start | bytes 688136 | tf_op jit(solution)/shard_map/while/body/eval_jaxpr/ppermute | solution.py:16
  64.1 11.3 %collective-permute-start.4 = (bf16[4,112,256]{2,1,0:T(8,128)(2,1)S(1)}, bf16[4,112,256]{2,1,0:T(8,128)(2,1)S(1)}, u32[]{:S(2)}, u32[]{:S(2)}) collective-permute-start(bf16[4,112,256]{2,1,0:T(8,128)(2,1)S(1)} %bitcast_dynamic-update-slice_fusion.29), channel_id=1, source_target_pairs={{0,64},{64,128},{128,192},{192,0},{1,65},{65,129},{129,193},{193,1... | collective-permute-start | bytes 688136 | tf_op jit(solution)/shard_map/while/body/eval_jaxpr/ppermute | solution.py:16
  65.6 11.4 %collective-permute-start.5 = (bf16[4,112,256]{2,1,0:T(8,128)(2,1)S(1)}, bf16[4,112,256]{2,1,0:T(8,128)(2,1)S(1)}, u32[]{:S(2)}, u32[]{:S(2)}) collective-permute-start(bf16[4,112,256]{2,1,0:T(8,128)(2,1)S(1)} %bitcast_dynamic-update-slice_fusion.29), channel_id=1, source_target_pairs={{0,192},{64,0},{128,64},{192,128},{1,193},{65,1},{129,65},{193,129... | collective-permute-start | bytes 688136 | tf_op jit(solution)/shard_map/while/body/eval_jaxpr/ppermute | solution.py:16
  68.7 11.4 %collective-permute-start.7 = (bf16[4,112,256]{2,1,0:T(8,128)(2,1)S(1)}, bf16[4,112,256]{2,1,0:T(8,128)(2,1)S(1)}, u32[]{:S(2)}, u32[]{:S(2)}) collective-permute-start(bf16[4,112,256]{2,1,0:T(8,128)(2,1)S(1)} %collective-permute-done.6), channel_id=1, source_target_pairs={{0,64},{64,128},{128,192},{192,0},{1,65},{65,129},{129,193},{193,1... | collective-permute-start | bytes 688136 | tf_op jit(solution)/shard_map/while/body/eval_jaxpr/ppermute | solution.py:16
  70.2 10.1 %collective-permute-start.8 = (bf16[4,112,256]{2,1,0:T(8,128)(2,1)S(1)}, bf16[4,112,256]{2,1,0:T(8,128)(2,1)S(1)}, u32[]{:S(2)}, u32[]{:S(2)}) collective-permute-start(bf16[4,112,256]{2,1,0:T(8,128)(2,1)S(1)} %collective-permute-done.6), channel_id=1, source_target_pairs={{0,192},{64,0},{128,64},{192,128},{1,193},{65,1},{129,65},{193,129... | collective-permute-start | bytes 688136 | tf_op jit(solution)/shard_map/while/body/eval_jaxpr/ppermute | solution.py:16
  72.1 8.2 %collective-permute-start.9 = (bf16[4,112,256]{2,1,0:T(8,128)(2,1)S(1)}, bf16[4,112,256]{2,1,0:T(8,128)(2,1)S(1)}, u32[]{:S(2)}, u32[]{:S(2)}) collective-permute-start(bf16[4,112,256]{2,1,0:T(8,128)(2,1)S(1)} %collective-permute-done.3), channel_id=1, source_target_pairs={{0,8},{8,0},{1,9},{9,1},{2,10},{10,2},{3,11},{11,3},{4,12},{12,4},... | collective-permute-start | bytes 688136 | tf_op jit(solution)/shard_map/while/body/eval_jaxpr/ppermute | solution.py:35
  84.7 8.6 %collective-permute-start.12 = (f32[104,256]{1,0:T(8,128)S(1)}, f32[104,256]{1,0:T(8,128)S(1)}, u32[]{:S(2)}, u32[]{:S(2)}) collective-permute-start(f32[104,256]{1,0:T(8,128)S(1)} %get-tuple-element.621), channel_id=1, source_target_pairs={{0,2},{2,4},{4,6},{6,0},{1,3},{3,5},{5,7},{7,1},{8,10},{10,12},{12... | collective-permute-start | bytes 319496 | tf_op jit(solution)/shard_map/while/body/eval_jaxpr/ppermute | solution.py:16
  106.0 10.0 %collective-permute-start.3 = (bf16[4,112,256]{2,1,0:T(8,128)(2,1)S(1)}, bf16[4,112,256]{2,1,0:T(8,128)(2,1)S(1)}, u32[]{:S(2)}, u32[]{:S(2)}) collective-permute-start(bf16[4,112,256]{2,1,0:T(8,128)(2,1)S(1)} %bitcast_dynamic-update-slice_fusion.29), channel_id=1, source_target_pairs={{0,128},{64,192},{128,0},{192,64},{1,129},{65,193},{129,1},{193,65... | collective-permute-start | bytes 688136 | tf_op jit(solution)/shard_map/while/body/eval_jaxpr/ppermute | solution.py:16
  108.0 11.4 %collective-permute-start.4 = (bf16[4,112,256]{2,1,0:T(8,128)(2,1)S(1)}, bf16[4,112,256]{2,1,0:T(8,128)(2,1)S(1)}, u32[]{:S(2)}, u32[]{:S(2)}) collective-permute-start(bf16[4,112,256]{2,1,0:T(8,128)(2,1)S(1)} %bitcast_dynamic-update-slice_fusion.29), channel_id=1, source_target_pairs={{0,64},{64,128},{128,192},{192,0},{1,65},{65,129},{129,193},{193,1... | collective-permute-start | bytes 688136 | tf_op jit(solution)/shard_map/while/body/eval_jaxpr/ppermute | solution.py:16
  108.6 11.0 %collective-permute-start.5 = (bf16[4,112,256]{2,1,0:T(8,128)(2,1)S(1)}, bf16[4,112,256]{2,1,0:T(8,128)(2,1)S(1)}, u32[]{:S(2)}, u32[]{:S(2)}) collective-permute-start(bf16[4,112,256]{2,1,0:T(8,128)(2,1)S(1)} %bitcast_dynamic-update-slice_fusion.29), channel_id=1, source_target_pairs={{0,192},{64,0},{128,64},{192,128},{1,193},{65,1},{129,65},{193,129... | collective-permute-start | bytes 688136 | tf_op jit(solution)/shard_map/while/body/eval_jaxpr/ppermute | solution.py:16
  111.3 10.8 %collective-permute-start.7 = (bf16[4,112,256]{2,1,0:T(8,128)(2,1)S(1)}, bf16[4,112,256]{2,1,0:T(8,128)(2,1)S(1)}, u32[]{:S(2)}, u32[]{:S(2)}) collective-permute-start(bf16[4,112,256]{2,1,0:T(8,128)(2,1)S(1)} %collective-permute-done.6), channel_id=1, source_target_pairs={{0,64},{64,128},{128,192},{192,0},{1,65},{65,129},{129,193},{193,1... | collective-permute-start | bytes 688136 | tf_op jit(solution)/shard_map/while/body/eval_jaxpr/ppermute | solution.py:16
  111.6 10.5 %collective-permute-start.8 = (bf16[4,112,256]{2,1,0:T(8,128)(2,1)S(1)}, bf16[4,112,256]{2,1,0:T(8,128)(2,1)S(1)}, u32[]{:S(2)}, u32[]{:S(2)}) collective-permute-start(bf16[4,112,256]{2,1,0:T(8,128)(2,1)S(1)} %collective-permute-done.6), channel_id=1, source_target_pairs={{0,192},{64,0},{128,64},{192,128},{1,193},{65,1},{129,65},{193,129... | collective-permute-start | bytes 688136 | tf_op jit(solution)/shard_map/while/body/eval_jaxpr/ppermute | solution.py:16
  129.7 8.2 %collective-permute-start.12 = (f32[104,256]{1,0:T(8,128)S(1)}, f32[104,256]{1,0:T(8,128)S(1)}, u32[]{:S(2)}, u32[]{:S(2)}) collective-permute-start(f32[104,256]{1,0:T(8,128)S(1)} %get-tuple-element.621), channel_id=1, source_target_pairs={{0,2},{2,4},{4,6},{6,0},{1,3},{3,5},{5,7},{7,1},{8,10},{10,12},{12... | collective-permute-start | bytes 319496 | tf_op jit(solution)/shard_map/while/body/eval_jaxpr/ppermute | solution.py:16
  129.7 8.2 %collective-permute-start.13 = (f32[104,256]{1,0:T(8,128)S(1)}, f32[104,256]{1,0:T(8,128)S(1)}, u32[]{:S(2)}, u32[]{:S(2)}) collective-permute-start(f32[104,256]{1,0:T(8,128)S(1)} %get-tuple-element.622), channel_id=1, source_target_pairs={{0,4},{2,6},{4,0},{6,2},{1,5},{3,7},{5,1},{7,3},{8,12},{10,14},{12... | collective-permute-start | bytes 319496 | tf_op jit(solution)/shard_map/while/body/eval_jaxpr/ppermute | solution.py:16
  147.2 18.9 %all-to-all-start.8 = ((f32[32,8,256]{2,1,0:T(8,128)}), f32[32,8,256]{2,1,0:T(8,128)S(1)}, u32[]{:S(2)}, u32[]{:S(2)}) async-start(f32[32,8,256]{2,1,0:T(8,128)} %broadcast_in_dim.299), calls=%async_computation.8 | async-start | bytes 524288 | tf_op jit(solution)/shard_map/all_to_all | solution.py:12
  (24 other events, 423.3 us)
where the time goes:
time: 169 us
  starting transfers between devices  79.4 us (47%)
  waiting for transfers between devices  60.8 us (36%)
  other arithmetic  8.75 us (5%)
  blocking collectives  8 us (5%)
  matrix products  5.91 us (3%)
  local copies, waits for them, and re-layouts  2.77 us (2%)
  between operations  2.1 us (1%)
    ppermute x33, starting transfers between devices, moved(): lax.ppermute(block, axis, [(i, (i + shift) % size) for i in range(size)])  66.2 us
    ppermute x33, waiting for transfers between devices, moved(): lax.ppermute(block, axis, [(i, (i + shift) % size) for i in range(size)])  42.4 us
    all_to_all x1, waiting for transfers between devices, spread(): lax.all_to_all(jnp.broadcast_to(block[None], (size,) + block.shape), axes...  12.1 us
    all_to_all x1, blocking collectives, spread(): lax.all_to_all(jnp.broadcast_to(block[None], (size,) + block.shape), axes...  8 us
    all_to_all x1, starting transfers between devices, spread(): lax.all_to_all(jnp.broadcast_to(block[None], (size,) + block.shape), axes...  6.71 us
    dot_general x3, matrix products, product(): jnp.einsum('cst,tk->csk', hessian, gathered, preferred_element_type=F32)  5.91 us
    ppermute x3, waiting for transfers between devices, scatter_rows(): half = mine + lax.ppermute(other, 'core', [(0, 1), (1, 0)])  4.9 us
    reduce_sum x3, other arithmetic, turn(): jnp.sum(jnp.where(on_diagonal, own_rows.astype(F32), 0.0), axis=1, keepdi...  4.42 us
  transfers between devices with their start and end apart: 43, of which 29 were waited for; matrix products, arithmetic and copies ran while one was open for 3% of the time, Pallas kernels for 0%

commit v1 on v0

--- a/solution.py
+++ b/solution.py
@@ -43,16 +43,18 @@
 
 
 def scatter_rows(partial_sum):
-    core = lax.axis_index("core")
-    place = lax.axis_index("x")
-    split = partial_sum.reshape((X, CORE) + partial_sum.shape[1:])
-    mine = lax.dynamic_index_in_dim(split, core, 1, keepdims=False)
-    other = lax.dynamic_index_in_dim(split, 1 - core, 1, keepdims=False)
-    half = mine + lax.ppermute(other, "core", [(0, 1), (1, 0)])
-    total = lax.dynamic_index_in_dim(half, place, 0, keepdims=False)
-    for shift in (2, 1, 3):
-        total = total + moved(lax.dynamic_index_in_dim(half, (place + shift) % X, 0, keepdims=False), "x", X, shift)
-    return total
+    core, place = lax.axis_index("core"), lax.axis_index("x")
+    split = partial_sum.reshape((X * CORE,) + partial_sum.shape[1:])
+
+    def of_chip(shift):
+        at = (place + shift) % X * CORE
+        other = lax.dynamic_index_in_dim(split, at + 1 - core, 0, keepdims=False)
+        return lax.dynamic_index_in_dim(split, at + core, 0, keepdims=False) + lax.ppermute(
+            other, "core", [(0, 1), (1, 0)]
+        )
+
+    parts = [moved(of_chip(shift), "x", X, shift) for shift in (2, 1, 3)]
+    return of_chip(0) + parts[0] + (parts[1] + parts[2])
 
 
 def gather_rows_seldom(block):

time: 169 us -> 168 us (level)
  starting transfers between devices: 79.4 us -> 83 us
  other arithmetic: 8.75 us -> 5.4 us
  waiting for transfers between devices: 60.8 us -> 58.3 us
    reduce_sum x3, other arithmetic: 4.42 us -> 1.15 us  [turn(): jnp.sum(jnp.where(on_diagonal, own_rows.astype(F32), 0.0), axis=1, keepdi...]
    ppermute x3 -> x12, starting transfers between devices: 0.28 us -> 3.3 us  [of_chip(): lax.ppermute(other, 'core', [(0, 1), (1, 0)])]
    ppermute x3 -> x12, waiting for transfers between devices: 4.9 us -> 2.4 us  [of_chip(): lax.ppermute(other, 'core', [(0, 1), (1, 0)])]
  transfers between devices with their start and end apart: 43 -> 52, of which waited for: 29 -> 37; matrix products, arithmetic and copies ran while one was open for 3% -> 1% of each run, Pallas kernels for 0% -> 0%
where the time goes in v1:
time: 168 us; the launch traced here: 167 us
  starting transfers between devices  83 us (49%)
  waiting for transfers between devices  58.3 us (35%)
  blocking collectives  8.73 us (5%)
  matrix products  5.91 us (4%)
  other arithmetic  5.4 us (3%)
  local copies, waits for them, and re-layouts  2.66 us (2%)
  between operations  2.1 us (1%)
    ppermute x33, starting transfers between devices, moved(): lax.ppermute(block, axis, [(i, (i + shift) % size) for i in range(size)])  66.5 us
    ppermute x33, waiting for transfers between devices, moved(): lax.ppermute(block, axis, [(i, (i + shift) % size) for i in range(size)])  43.6 us
    all_to_all x1, waiting for transfers between devices, spread(): lax.all_to_all(jnp.broadcast_to(block[None], (size,) + block.shape), axes...  12.1 us
    all_to_all x1, blocking collectives, spread(): lax.all_to_all(jnp.broadcast_to(block[None], (size,) + block.shape), axes...  8.73 us
    all_to_all x1, starting transfers between devices, spread(): lax.all_to_all(jnp.broadcast_to(block[None], (size,) + block.shape), axes...  7.18 us
    dot_general x3, matrix products, product(): jnp.einsum('cst,tk->csk', hessian, gathered, preferred_element_type=F32)  5.91 us
    ppermute x3, starting transfers between devices, gather_rows(): other[2] = lax.ppermute(mine[2], 'zp', swap)  4.6 us
  transfers between devices with their start and end apart: 52, of which 37 were waited for; matrix products, arithmetic and copies ran while one was open for 1% of the time, Pallas kernels for 0%

profile of v1, /device:TPU:32, one launch (start us, length us, event | category | flops | bytes accessed | tf_op | source)
XLA Modules:
  0.0 167.4 jit_solution(849201027554669351)
XLA Ops:
  2.4 133.1 %while.25 = (s32[]{:T(128)}, bf16[112,256]{1,0:T(8,128)(2,1)S(1)}, f32[3,104,256]{2,1,0:T(8,128)S(1)}, f32[8,104,256]{2,1,0:T(8,128)S(1)}, f32[256]{0:T(256)S(1)...) while((s32[]{:T(128)}, bf16[112,256]{1,0:T(8,128)(2,1)S(1)}, ...), condition=%wide.region_5.6_spmd.clone, body=%wide.region_0.5_spmd.clone.sunk | while | flops 1420384896 | bytes 55856980 | solution.py:118
  2.4 6.4 %collective-permute-start = (bf16[112,256]{1,0:T(8,128)(2,1)S(1)}, bf16[112,256]{1,0:T(8,128)(2,1)S(1)}, u32[]{:S(2)}, u32[]{:S(2)}) collective-permute-start(bf16[112,256]{1,0:T(8,128)(2,1)S(1)} %get-tuple-element.661), channel_id=1, source_target_pairs={{0,32},{16,48},{32,0},{48,16},{1,33},{17,49},{33,1},{49,17},{2,34}... | collective-permute-start | bytes 172040 | tf_op jit(solution)/shard_map/while/body/eval_jaxpr/ppermute | solution.py:16
  10.2 2.7 %collective-permute-start.2 = (bf16[112,256]{1,0:T(8,128)(2,1)S(1)}, bf16[112,256]{1,0:T(8,128)(2,1)S(1)}, u32[]{:S(2)}, u32[]{:S(2)}) collective-permute-start(bf16[112,256]{1,0:T(8,128)(2,1)S(1)} %get-tuple-element.661), channel_id=1, source_target_pairs={{0,48},{16,0},{32,16},{48,32},{1,49},{17,1},{33,17},{49,33},{2,50}... | collective-permute-start | bytes 172040 | tf_op jit(solution)/shard_map/while/body/eval_jaxpr/ppermute | solution.py:16
  13.0 3.0 %collective-permute-done.1 = bf16[112,256]{1,0:T(8,128)(2,1)S(1)} collective-permute-done((bf16[112,256]{1,0:T(8,128)(2,1)S(1)}, bf16[112,256]{1,0:T(8,128)(2,1)S(1)}, u32[]{:S(2)}, u32[]{:S(2)}) %collective-permute-start.1) | collective-permute-done | bytes 57376 | tf_op jit(solution)/shard_map/while/body/eval_jaxpr/ppermute | solution.py:16
  16.6 3.2 %collective-permute-start.3 = (bf16[4,112,256]{2,1,0:T(8,128)(2,1)S(1)}, bf16[4,112,256]{2,1,0:T(8,128)(2,1)S(1)}, u32[]{:S(2)}, u32[]{:S(2)}) collective-permute-start(bf16[4,112,256]{2,1,0:T(8,128)(2,1)S(1)} %bitcast_dynamic-update-slice_fusion.29), channel_id=1, source_target_pairs={{0,128},{64,192},{128,0},{192,64},{1,129},{65,193},{129,1},{193,65... | collective-permute-start | bytes 688136 | tf_op jit(solution)/shard_map/while/body/eval_jaxpr/ppermute | solution.py:16
  20.7 2.6 %collective-permute-start.5 = (bf16[4,112,256]{2,1,0:T(8,128)(2,1)S(1)}, bf16[4,112,256]{2,1,0:T(8,128)(2,1)S(1)}, u32[]{:S(2)}, u32[]{:S(2)}) collective-permute-start(bf16[4,112,256]{2,1,0:T(8,128)(2,1)S(1)} %bitcast_dynamic-update-slice_fusion.29), channel_id=1, source_target_pairs={{0,192},{64,0},{128,64},{192,128},{1,193},{65,1},{129,65},{193,129... | collective-permute-start | bytes 688136 | tf_op jit(solution)/shard_map/while/body/eval_jaxpr/ppermute | solution.py:16
  23.6 2.9 %collective-permute-start.8 = (bf16[4,112,256]{2,1,0:T(8,128)(2,1)S(1)}, bf16[4,112,256]{2,1,0:T(8,128)(2,1)S(1)}, u32[]{:S(2)}, u32[]{:S(2)}) collective-permute-start(bf16[4,112,256]{2,1,0:T(8,128)(2,1)S(1)} %collective-permute-done.6), channel_id=1, source_target_pairs={{0,192},{64,0},{128,64},{192,128},{1,193},{65,1},{129,65},{193,129... | collective-permute-start | bytes 688136 | tf_op jit(solution)/shard_map/while/body/eval_jaxpr/ppermute | solution.py:16
  28.5 2.2 %collective-permute-done.4 = bf16[4,112,256]{2,1,0:T(8,128)(2,1)S(1)} collective-permute-done((bf16[4,112,256]{2,1,0:T(8,128)(2,1)S(1)}, bf16[4,112,256]{2,1,0:T(8,128)(2,1)S(1)}, u32[]{:S(2)}, u32[]{:S(2)}) %collective-permute-start.4) | collective-permute-done | bytes 229408 | tf_op jit(solution)/shard_map/while/body/eval_jaxpr/ppermute | solution.py:16
  31.7 2.3 %collective-permute-done.7 = bf16[4,112,256]{2,1,0:T(8,128)(2,1)S(1)} collective-permute-done((bf16[4,112,256]{2,1,0:T(8,128)(2,1)S(1)}, bf16[4,112,256]{2,1,0:T(8,128)(2,1)S(1)}, u32[]{:S(2)}, u32[]{:S(2)}) %collective-permute-start.7) | collective-permute-done | bytes 229408 | tf_op jit(solution)/shard_map/while/body/eval_jaxpr/ppermute | solution.py:16
  48.3 4.8 %collective-permute-start = (bf16[112,256]{1,0:T(8,128)(2,1)S(1)}, bf16[112,256]{1,0:T(8,128)(2,1)S(1)}, u32[]{:S(2)}, u32[]{:S(2)}) collective-permute-start(bf16[112,256]{1,0:T(8,128)(2,1)S(1)} %get-tuple-element.661), channel_id=1, source_target_pairs={{0,32},{16,48},{32,0},{48,16},{1,33},{17,49},{33,1},{49,17},{2,34}... | collective-permute-start | bytes 172040 | tf_op jit(solution)/shard_map/while/body/eval_jaxpr/ppermute | solution.py:16
  54.7 2.5 %collective-permute-start.2 = (bf16[112,256]{1,0:T(8,128)(2,1)S(1)}, bf16[112,256]{1,0:T(8,128)(2,1)S(1)}, u32[]{:S(2)}, u32[]{:S(2)}) collective-permute-start(bf16[112,256]{1,0:T(8,128)(2,1)S(1)} %get-tuple-element.661), channel_id=1, source_target_pairs={{0,48},{16,0},{32,16},{48,32},{1,49},{17,1},{33,17},{49,33},{2,50}... | collective-permute-start | bytes 172040 | tf_op jit(solution)/shard_map/while/body/eval_jaxpr/ppermute | solution.py:16
  57.3 2.6 %collective-permute-done.1 = bf16[112,256]{1,0:T(8,128)(2,1)S(1)} collective-permute-done((bf16[112,256]{1,0:T(8,128)(2,1)S(1)}, bf16[112,256]{1,0:T(8,128)(2,1)S(1)}, u32[]{:S(2)}, u32[]{:S(2)}) %collective-permute-start.1) | collective-permute-done | bytes 57376 | tf_op jit(solution)/shard_map/while/body/eval_jaxpr/ppermute | solution.py:16
  60.5 2.4 %collective-permute-start.3 = (bf16[4,112,256]{2,1,0:T(8,128)(2,1)S(1)}, bf16[4,112,256]{2,1,0:T(8,128)(2,1)S(1)}, u32[]{:S(2)}, u32[]{:S(2)}) collective-permute-start(bf16[4,112,256]{2,1,0:T(8,128)(2,1)S(1)} %bitcast_dynamic-update-slice_fusion.29), channel_id=1, source_target_pairs={{0,128},{64,192},{128,0},{192,64},{1,129},{65,193},{129,1},{193,65... | collective-permute-start | bytes 688136 | tf_op jit(solution)/shard_map/while/body/eval_jaxpr/ppermute | solution.py:16
  75.6 2.6 %collective-permute-done.7 = bf16[4,112,256]{2,1,0:T(8,128)(2,1)S(1)} collective-permute-done((bf16[4,112,256]{2,1,0:T(8,128)(2,1)S(1)}, bf16[4,112,256]{2,1,0:T(8,128)(2,1)S(1)}, u32[]{:S(2)}, u32[]{:S(2)}) %collective-permute-start.7) | collective-permute-done | bytes 229408 | tf_op jit(solution)/shard_map/while/body/eval_jaxpr/ppermute | solution.py:16
  86.5 2.3 %collective-permute-done.13 = f32[104,256]{1,0:T(8,128)S(1)} collective-permute-done((f32[104,256]{1,0:T(8,128)S(1)}, f32[104,256]{1,0:T(8,128)S(1)}, u32[]{:S(2)}, u32[]{:S(2)}) %collective-permute-start.13) | collective-permute-done | bytes 106528 | tf_op jit(solution)/shard_map/while/body/eval_jaxpr/ppermute | solution.py:16
  92.3 3.5 %collective-permute-start = (bf16[112,256]{1,0:T(8,128)(2,1)S(1)}, bf16[112,256]{1,0:T(8,128)(2,1)S(1)}, u32[]{:S(2)}, u32[]{:S(2)}) collective-permute-start(bf16[112,256]{1,0:T(8,128)(2,1)S(1)} %get-tuple-element.661), channel_id=1, source_target_pairs={{0,32},{16,48},{32,0},{48,16},{1,33},{17,49},{33,1},{49,17},{2,34}... | collective-permute-start | bytes 172040 | tf_op jit(solution)/shard_map/while/body/eval_jaxpr/ppermute | solution.py:16
  97.6 2.3 %collective-permute-start.2 = (bf16[112,256]{1,0:T(8,128)(2,1)S(1)}, bf16[112,256]{1,0:T(8,128)(2,1)S(1)}, u32[]{:S(2)}, u32[]{:S(2)}) collective-permute-start(bf16[112,256]{1,0:T(8,128)(2,1)S(1)} %get-tuple-element.661), channel_id=1, source_target_pairs={{0,48},{16,0},{32,16},{48,32},{1,49},{17,1},{33,17},{49,33},{2,50}... | collective-permute-start | bytes 172040 | tf_op jit(solution)/shard_map/while/body/eval_jaxpr/ppermute | solution.py:16
  110.4 2.2 %collective-permute-start.8 = (bf16[4,112,256]{2,1,0:T(8,128)(2,1)S(1)}, bf16[4,112,256]{2,1,0:T(8,128)(2,1)S(1)}, u32[]{:S(2)}, u32[]{:S(2)}) collective-permute-start(bf16[4,112,256]{2,1,0:T(8,128)(2,1)S(1)} %collective-permute-done.6), channel_id=1, source_target_pairs={{0,192},{64,0},{128,64},{192,128},{1,193},{65,1},{129,65},{193,129... | collective-permute-start | bytes 688136 | tf_op jit(solution)/shard_map/while/body/eval_jaxpr/ppermute | solution.py:16
  117.6 3.7 %collective-permute-done.7 = bf16[4,112,256]{2,1,0:T(8,128)(2,1)S(1)} collective-permute-done((bf16[4,112,256]{2,1,0:T(8,128)(2,1)S(1)}, bf16[4,112,256]{2,1,0:T(8,128)(2,1)S(1)}, u32[]{:S(2)}, u32[]{:S(2)}) %collective-permute-start.7) | collective-permute-done | bytes 229408 | tf_op jit(solution)/shard_map/while/body/eval_jaxpr/ppermute | solution.py:16
  126.1 2.8 %collective-permute-start.14 = (f32[104,256]{1,0:T(8,128)S(1)}, f32[104,256]{1,0:T(8,128)S(1)}, u32[]{:S(2)}, u32[]{:S(2)}) collective-permute-start(f32[104,256]{1,0:T(8,128)S(1)} %get-tuple-element.629), channel_id=1, source_target_pairs={{0,6},{2,0},{4,2},{6,4},{1,7},{3,1},{5,3},{7,5},{8,14},{10,8},{12,... | collective-permute-start | bytes 319496 | tf_op jit(solution)/shard_map/while/body/eval_jaxpr/ppermute | solution.py:16
  129.6 2.3 %collective-permute-done.13 = f32[104,256]{1,0:T(8,128)S(1)} collective-permute-done((f32[104,256]{1,0:T(8,128)S(1)}, f32[104,256]{1,0:T(8,128)S(1)}, u32[]{:S(2)}, u32[]{:S(2)}) %collective-permute-start.13) | collective-permute-done | bytes 106528 | tf_op jit(solution)/shard_map/while/body/eval_jaxpr/ppermute | solution.py:16
  135.7 8.7 %all_to_all.45 = f32[8,8,256]{2,1,0:T(8,128)S(1)} all-to-all(f32[8,8,256]{2,1,0:T(8,128)S(1)} %broadcast_in_dim.298), channel_id=1, replica_groups=mesh['y'=4,'zs'=4,'zp'=2,'x'=4,'core'=2] {'x','core'}, dimensions={0} | all-to-all | bytes 131072 | tf_op jit(solution)/shard_map/all_to_all | solution.py:12
  145.1 7.2 %all-to-all-start.8 = ((f32[32,8,256]{2,1,0:T(8,128)}), f32[32,8,256]{2,1,0:T(8,128)S(1)}, u32[]{:S(2)}, u32[]{:S(2)}) async-start(f32[32,8,256]{2,1,0:T(8,128)} %broadcast_in_dim.299), calls=%async_computation.8 | async-start | bytes 524288 | tf_op jit(solution)/shard_map/all_to_all | solution.py:12
  152.4 12.1 %all-to-all-done.8 = f32[32,8,256]{2,1,0:T(8,128)S(1)} async-done(((f32[32,8,256]{2,1,0:T(8,128)}), f32[32,8,256]{2,1,0:T(8,128)S(1)}, u32[]{:S(2)}, u32[]{:S(2)}) %all-to-all-start.8) | async-done | bytes 262176 | tf_op jit(solution)/shard_map/all_to_all | solution.py:12
  (207 shorter events, 76.9 us)
Async XLA Ops:
  2.4 10.6 %collective-permute-start = (bf16[112,256]{1,0:T(8,128)(2,1)S(1)}, bf16[112,256]{1,0:T(8,128)(2,1)S(1)}, u32[]{:S(2)}, u32[]{:S(2)}) collective-permute-start(bf16[112,256]{1,0:T(8,128)(2,1)S(1)} %get-tuple-element.661), channel_id=1, source_target_pairs={{0,32},{16,48},{32,0},{48,16},{1,33},{17,49},{33,1},{49,17},{2,34}... | collective-permute-start | bytes 172040 | tf_op jit(solution)/shard_map/while/body/eval_jaxpr/ppermute | solution.py:16
  8.8 7.3 %collective-permute-start.1 = (bf16[112,256]{1,0:T(8,128)(2,1)S(1)}, bf16[112,256]{1,0:T(8,128)(2,1)S(1)}, u32[]{:S(2)}, u32[]{:S(2)}) collective-permute-start(bf16[112,256]{1,0:T(8,128)(2,1)S(1)} %get-tuple-element.661), channel_id=1, source_target_pairs={{0,16},{16,32},{32,48},{48,0},{1,17},{17,33},{33,49},{49,1},{2,18}... | collective-permute-start | bytes 172040 | tf_op jit(solution)/shard_map/while/body/eval_jaxpr/ppermute | solution.py:16
  16.6 10.0 %collective-permute-start.3 = (bf16[4,112,256]{2,1,0:T(8,128)(2,1)S(1)}, bf16[4,112,256]{2,1,0:T(8,128)(2,1)S(1)}, u32[]{:S(2)}, u32[]{:S(2)}) collective-permute-start(bf16[4,112,256]{2,1,0:T(8,128)(2,1)S(1)} %bitcast_dynamic-update-slice_fusion.29), channel_id=1, source_target_pairs={{0,128},{64,192},{128,0},{192,64},{1,129},{65,193},{129,1},{193,65... | collective-permute-start | bytes 688136 | tf_op jit(solution)/shard_map/while/body/eval_jaxpr/ppermute | solution.py:16
  19.9 10.8 %collective-permute-start.4 = (bf16[4,112,256]{2,1,0:T(8,128)(2,1)S(1)}, bf16[4,112,256]{2,1,0:T(8,128)(2,1)S(1)}, u32[]{:S(2)}, u32[]{:S(2)}) collective-permute-start(bf16[4,112,256]{2,1,0:T(8,128)(2,1)S(1)} %bitcast_dynamic-update-slice_fusion.29), channel_id=1, source_target_pairs={{0,64},{64,128},{128,192},{192,0},{1,65},{65,129},{129,193},{193,1... | collective-permute-start | bytes 688136 | tf_op jit(solution)/shard_map/while/body/eval_jaxpr/ppermute | solution.py:16
  20.7 11.0 %collective-permute-start.5 = (bf16[4,112,256]{2,1,0:T(8,128)(2,1)S(1)}, bf16[4,112,256]{2,1,0:T(8,128)(2,1)S(1)}, u32[]{:S(2)}, u32[]{:S(2)}) collective-permute-start(bf16[4,112,256]{2,1,0:T(8,128)(2,1)S(1)} %bitcast_dynamic-update-slice_fusion.29), channel_id=1, source_target_pairs={{0,192},{64,0},{128,64},{192,128},{1,193},{65,1},{129,65},{193,129... | collective-permute-start | bytes 688136 | tf_op jit(solution)/shard_map/while/body/eval_jaxpr/ppermute | solution.py:16
  23.2 10.9 %collective-permute-start.7 = (bf16[4,112,256]{2,1,0:T(8,128)(2,1)S(1)}, bf16[4,112,256]{2,1,0:T(8,128)(2,1)S(1)}, u32[]{:S(2)}, u32[]{:S(2)}) collective-permute-start(bf16[4,112,256]{2,1,0:T(8,128)(2,1)S(1)} %collective-permute-done.6), channel_id=1, source_target_pairs={{0,64},{64,128},{128,192},{192,0},{1,65},{65,129},{129,193},{193,1... | collective-permute-start | bytes 688136 | tf_op jit(solution)/shard_map/while/body/eval_jaxpr/ppermute | solution.py:16
  23.6 10.6 %collective-permute-start.8 = (bf16[4,112,256]{2,1,0:T(8,128)(2,1)S(1)}, bf16[4,112,256]{2,1,0:T(8,128)(2,1)S(1)}, u32[]{:S(2)}, u32[]{:S(2)}) collective-permute-start(bf16[4,112,256]{2,1,0:T(8,128)(2,1)S(1)} %collective-permute-done.6), channel_id=1, source_target_pairs={{0,192},{64,0},{128,64},{192,128},{1,193},{65,1},{129,65},{193,129... | collective-permute-start | bytes 688136 | tf_op jit(solution)/shard_map/while/body/eval_jaxpr/ppermute | solution.py:16
  26.7 7.5 %collective-permute-start.9 = (bf16[4,112,256]{2,1,0:T(8,128)(2,1)S(1)}, bf16[4,112,256]{2,1,0:T(8,128)(2,1)S(1)}, u32[]{:S(2)}, u32[]{:S(2)}) collective-permute-start(bf16[4,112,256]{2,1,0:T(8,128)(2,1)S(1)} %collective-permute-done.3), channel_id=1, source_target_pairs={{0,8},{8,0},{1,9},{9,1},{2,10},{10,2},{3,11},{11,3},{4,12},{12,4},... | collective-permute-start | bytes 688136 | tf_op jit(solution)/shard_map/while/body/eval_jaxpr/ppermute | solution.py:35
  48.3 9.0 %collective-permute-start = (bf16[112,256]{1,0:T(8,128)(2,1)S(1)}, bf16[112,256]{1,0:T(8,128)(2,1)S(1)}, u32[]{:S(2)}, u32[]{:S(2)}) collective-permute-start(bf16[112,256]{1,0:T(8,128)(2,1)S(1)} %get-tuple-element.661), channel_id=1, source_target_pairs={{0,32},{16,48},{32,0},{48,16},{1,33},{17,49},{33,1},{49,17},{2,34}... | collective-permute-start | bytes 172040 | tf_op jit(solution)/shard_map/while/body/eval_jaxpr/ppermute | solution.py:16
  60.5 10.1 %collective-permute-start.3 = (bf16[4,112,256]{2,1,0:T(8,128)(2,1)S(1)}, bf16[4,112,256]{2,1,0:T(8,128)(2,1)S(1)}, u32[]{:S(2)}, u32[]{:S(2)}) collective-permute-start(bf16[4,112,256]{2,1,0:T(8,128)(2,1)S(1)} %bitcast_dynamic-update-slice_fusion.29), channel_id=1, source_target_pairs={{0,128},{64,192},{128,0},{192,64},{1,129},{65,193},{129,1},{193,65... | collective-permute-start | bytes 688136 | tf_op jit(solution)/shard_map/while/body/eval_jaxpr/ppermute | solution.py:16
  63.0 11.2 %collective-permute-start.4 = (bf16[4,112,256]{2,1,0:T(8,128)(2,1)S(1)}, bf16[4,112,256]{2,1,0:T(8,128)(2,1)S(1)}, u32[]{:S(2)}, u32[]{:S(2)}) collective-permute-start(bf16[4,112,256]{2,1,0:T(8,128)(2,1)S(1)} %bitcast_dynamic-update-slice_fusion.29), channel_id=1, source_target_pairs={{0,64},{64,128},{128,192},{192,0},{1,65},{65,129},{129,193},{193,1... | collective-permute-start | bytes 688136 | tf_op jit(solution)/shard_map/while/body/eval_jaxpr/ppermute | solution.py:16
  64.4 11.2 %collective-permute-start.5 = (bf16[4,112,256]{2,1,0:T(8,128)(2,1)S(1)}, bf16[4,112,256]{2,1,0:T(8,128)(2,1)S(1)}, u32[]{:S(2)}, u32[]{:S(2)}) collective-permute-start(bf16[4,112,256]{2,1,0:T(8,128)(2,1)S(1)} %bitcast_dynamic-update-slice_fusion.29), channel_id=1, source_target_pairs={{0,192},{64,0},{128,64},{192,128},{1,193},{65,1},{129,65},{193,129... | collective-permute-start | bytes 688136 | tf_op jit(solution)/shard_map/while/body/eval_jaxpr/ppermute | solution.py:16
  66.5 11.7 %collective-permute-start.7 = (bf16[4,112,256]{2,1,0:T(8,128)(2,1)S(1)}, bf16[4,112,256]{2,1,0:T(8,128)(2,1)S(1)}, u32[]{:S(2)}, u32[]{:S(2)}) collective-permute-start(bf16[4,112,256]{2,1,0:T(8,128)(2,1)S(1)} %collective-permute-done.6), channel_id=1, source_target_pairs={{0,64},{64,128},{128,192},{192,0},{1,65},{65,129},{129,193},{193,1... | collective-permute-start | bytes 688136 | tf_op jit(solution)/shard_map/while/body/eval_jaxpr/ppermute | solution.py:16
  68.1 10.2 %collective-permute-start.8 = (bf16[4,112,256]{2,1,0:T(8,128)(2,1)S(1)}, bf16[4,112,256]{2,1,0:T(8,128)(2,1)S(1)}, u32[]{:S(2)}, u32[]{:S(2)}) collective-permute-start(bf16[4,112,256]{2,1,0:T(8,128)(2,1)S(1)} %collective-permute-done.6), channel_id=1, source_target_pairs={{0,192},{64,0},{128,64},{192,128},{1,193},{65,1},{129,65},{193,129... | collective-permute-start | bytes 688136 | tf_op jit(solution)/shard_map/while/body/eval_jaxpr/ppermute | solution.py:16
  70.6 7.7 %collective-permute-start.9 = (bf16[4,112,256]{2,1,0:T(8,128)(2,1)S(1)}, bf16[4,112,256]{2,1,0:T(8,128)(2,1)S(1)}, u32[]{:S(2)}, u32[]{:S(2)}) collective-permute-start(bf16[4,112,256]{2,1,0:T(8,128)(2,1)S(1)} %collective-permute-done.3), channel_id=1, source_target_pairs={{0,8},{8,0},{1,9},{9,1},{2,10},{10,2},{3,11},{11,3},{4,12},{12,4},... | collective-permute-start | bytes 688136 | tf_op jit(solution)/shard_map/while/body/eval_jaxpr/ppermute | solution.py:35
  92.3 8.4 %collective-permute-start = (bf16[112,256]{1,0:T(8,128)(2,1)S(1)}, bf16[112,256]{1,0:T(8,128)(2,1)S(1)}, u32[]{:S(2)}, u32[]{:S(2)}) collective-permute-start(bf16[112,256]{1,0:T(8,128)(2,1)S(1)} %get-tuple-element.661), channel_id=1, source_target_pairs={{0,32},{16,48},{32,0},{48,16},{1,33},{17,49},{33,1},{49,17},{2,34}... | collective-permute-start | bytes 172040 | tf_op jit(solution)/shard_map/while/body/eval_jaxpr/ppermute | solution.py:16
  104.1 10.0 %collective-permute-start.3 = (bf16[4,112,256]{2,1,0:T(8,128)(2,1)S(1)}, bf16[4,112,256]{2,1,0:T(8,128)(2,1)S(1)}, u32[]{:S(2)}, u32[]{:S(2)}) collective-permute-start(bf16[4,112,256]{2,1,0:T(8,128)(2,1)S(1)} %bitcast_dynamic-update-slice_fusion.29), channel_id=1, source_target_pairs={{0,128},{64,192},{128,0},{192,64},{1,129},{65,193},{129,1},{193,65... | collective-permute-start | bytes 688136 | tf_op jit(solution)/shard_map/while/body/eval_jaxpr/ppermute | solution.py:16
  106.0 11.5 %collective-permute-start.4 = (bf16[4,112,256]{2,1,0:T(8,128)(2,1)S(1)}, bf16[4,112,256]{2,1,0:T(8,128)(2,1)S(1)}, u32[]{:S(2)}, u32[]{:S(2)}) collective-permute-start(bf16[4,112,256]{2,1,0:T(8,128)(2,1)S(1)} %bitcast_dynamic-update-slice_fusion.29), channel_id=1, source_target_pairs={{0,64},{64,128},{128,192},{192,0},{1,65},{65,129},{129,193},{193,1... | collective-permute-start | bytes 688136 | tf_op jit(solution)/shard_map/while/body/eval_jaxpr/ppermute | solution.py:16
  107.3 10.1 %collective-permute-start.5 = (bf16[4,112,256]{2,1,0:T(8,128)(2,1)S(1)}, bf16[4,112,256]{2,1,0:T(8,128)(2,1)S(1)}, u32[]{:S(2)}, u32[]{:S(2)}) collective-permute-start(bf16[4,112,256]{2,1,0:T(8,128)(2,1)S(1)} %bitcast_dynamic-update-slice_fusion.29), channel_id=1, source_target_pairs={{0,192},{64,0},{128,64},{192,128},{1,193},{65,1},{129,65},{193,129... | collective-permute-start | bytes 688136 | tf_op jit(solution)/shard_map/while/body/eval_jaxpr/ppermute | solution.py:16
  109.3 11.9 %collective-permute-start.7 = (bf16[4,112,256]{2,1,0:T(8,128)(2,1)S(1)}, bf16[4,112,256]{2,1,0:T(8,128)(2,1)S(1)}, u32[]{:S(2)}, u32[]{:S(2)}) collective-permute-start(bf16[4,112,256]{2,1,0:T(8,128)(2,1)S(1)} %collective-permute-done.6), channel_id=1, source_target_pairs={{0,64},{64,128},{128,192},{192,0},{1,65},{65,129},{129,193},{193,1... | collective-permute-start | bytes 688136 | tf_op jit(solution)/shard_map/while/body/eval_jaxpr/ppermute | solution.py:16
  110.4 10.9 %collective-permute-start.8 = (bf16[4,112,256]{2,1,0:T(8,128)(2,1)S(1)}, bf16[4,112,256]{2,1,0:T(8,128)(2,1)S(1)}, u32[]{:S(2)}, u32[]{:S(2)}) collective-permute-start(bf16[4,112,256]{2,1,0:T(8,128)(2,1)S(1)} %collective-permute-done.6), channel_id=1, source_target_pairs={{0,192},{64,0},{128,64},{192,128},{1,193},{65,1},{129,65},{193,129... | collective-permute-start | bytes 688136 | tf_op jit(solution)/shard_map/while/body/eval_jaxpr/ppermute | solution.py:16
  114.1 7.2 %collective-permute-start.9 = (bf16[4,112,256]{2,1,0:T(8,128)(2,1)S(1)}, bf16[4,112,256]{2,1,0:T(8,128)(2,1)S(1)}, u32[]{:S(2)}, u32[]{:S(2)}) collective-permute-start(bf16[4,112,256]{2,1,0:T(8,128)(2,1)S(1)} %collective-permute-done.3), channel_id=1, source_target_pairs={{0,8},{8,0},{1,9},{9,1},{2,10},{10,2},{3,11},{11,3},{4,12},{12,4},... | collective-permute-start | bytes 688136 | tf_op jit(solution)/shard_map/while/body/eval_jaxpr/ppermute | solution.py:35
  126.1 7.4 %collective-permute-start.14 = (f32[104,256]{1,0:T(8,128)S(1)}, f32[104,256]{1,0:T(8,128)S(1)}, u32[]{:S(2)}, u32[]{:S(2)}) collective-permute-start(f32[104,256]{1,0:T(8,128)S(1)} %get-tuple-element.629), channel_id=1, source_target_pairs={{0,6},{2,0},{4,2},{6,4},{1,7},{3,1},{5,3},{7,5},{8,14},{10,8},{12,... | collective-permute-start | bytes 319496 | tf_op jit(solution)/shard_map/while/body/eval_jaxpr/ppermute | solution.py:16
  145.1 19.4 %all-to-all-start.8 = ((f32[32,8,256]{2,1,0:T(8,128)}), f32[32,8,256]{2,1,0:T(8,128)S(1)}, u32[]{:S(2)}, u32[]{:S(2)}) async-start(f32[32,8,256]{2,1,0:T(8,128)} %broadcast_in_dim.299), calls=%async_computation.8 | async-start | bytes 524288 | tf_op jit(solution)/shard_map/all_to_all | solution.py:12
  (33 other events, 440.0 us)

commit v2 on v1

--- a/solution.py
+++ b/solution.py
@@ -71,8 +71,9 @@
 def total_sums(rows):
     sums = jnp.stack([jnp.sum(first * second, axis=0) for first, second in rows])
     sums = jnp.pad(sums, ((0, 8 - len(rows)), (0, 0)))
-    sums = jnp.sum(spread(sums, ("x", "core"), X * CORE), axis=0)
-    return jnp.sum(spread(sums, ("y", "zs", "zp"), Y * ZS * ZP), axis=0)
+    sums = sums + lax.ppermute(sums, "core", [(0, 1), (1, 0)])
+    sums = jnp.sum(spread(sums, ("y", "x"), Y * X), axis=0)
+    return jnp.sum(spread(sums, ("zs", "zp"), ZS * ZP), axis=0)
 
 
 def on_device(hessian, exponents, masks, weights):

time: 168 us -> 167 us (level)
  blocking collectives: 8.73 us -> 13.3 us
  waiting for transfers between devices: 58.3 us -> 54.3 us
    all_to_all x1, waiting for transfers between devices: 12.1 us -> 6.84 us  [spread(): lax.all_to_all(jnp.broadcast_to(block[None], (size,) + block.shape), axes...]
    all_to_all x1, blocking collectives: 8.73 us -> 13.3 us  [spread(): lax.all_to_all(jnp.broadcast_to(block[None], (size,) + block.shape), axes...]
    all_to_all x1, starting transfers between devices: 7.18 us -> 5.32 us  [spread(): lax.all_to_all(jnp.broadcast_to(block[None], (size,) + block.shape), axes...]
  transfers between devices with their start and end apart: 52 -> 53, of which waited for: 37 -> 39; matrix products, arithmetic and copies ran while one was open for 1% -> 1% of each run, Pallas kernels for 0% -> 0%
where the time goes in v2:
time: 167 us; the launch traced here: 166 us
  starting transfers between devices  81.4 us (49%)
  waiting for transfers between devices  54.3 us (33%)
  blocking collectives  13.3 us (8%)
  matrix products  5.91 us (4%)
  other arithmetic  5.39 us (3%)
  local copies, waits for them, and re-layouts  2.59 us (2%)
  between operations  2.1 us (1%)
    ppermute x33, starting transfers between devices, moved(): lax.ppermute(block, axis, [(i, (i + shift) % size) for i in range(size)])  66.5 us
    ppermute x33, waiting for transfers between devices, moved(): lax.ppermute(block, axis, [(i, (i + shift) % size) for i in range(size)])  43.7 us
    all_to_all x1, blocking collectives, spread(): lax.all_to_all(jnp.broadcast_to(block[None], (size,) + block.shape), axes...  13.3 us
    all_to_all x1, waiting for transfers between devices, spread(): lax.all_to_all(jnp.broadcast_to(block[None], (size,) + block.shape), axes...  6.84 us
    dot_general x3, matrix products, product(): jnp.einsum('cst,tk->csk', hessian, gathered, preferred_element_type=F32)  5.91 us
    all_to_all x1, starting transfers between devices, spread(): lax.all_to_all(jnp.broadcast_to(block[None], (size,) + block.shape), axes...  5.32 us
    ppermute x3, starting transfers between devices, gather_rows(): other[2] = lax.ppermute(mine[2], 'zp', swap)  4.02 us
  transfers between devices with their start and end apart: 53, of which 39 were waited for; matrix products, arithmetic and copies ran while one was open for 1% of the time, Pallas kernels for 0%

profile of v2, /device:TPU:32, one launch (start us, length us, event | category | flops | bytes accessed | tf_op | source)
XLA Modules:
  0.0 166.1 jit_solution(2093383546661923809)
XLA Ops:
  2.4 133.3 %while.25 = (s32[]{:T(128)}, bf16[112,256]{1,0:T(8,128)(2,1)S(1)}, f32[3,104,256]{2,1,0:T(8,128)S(1)}, f32[8,104,256]{2,1,0:T(8,128)S(1)}, f32[256]{0:T(256)S(1)...) while((s32[]{:T(128)}, bf16[112,256]{1,0:T(8,128)(2,1)S(1)}, ...), condition=%wide.region_5.6_spmd.clone, body=%wide.region_0.5_spmd.clone.sunk | while | flops 1420384896 | bytes 55856980 | solution.py:119
  2.4 6.4 %collective-permute-start.2 = (bf16[112,256]{1,0:T(8,128)(2,1)S(1)}, bf16[112,256]{1,0:T(8,128)(2,1)S(1)}, u32[]{:S(2)}, u32[]{:S(2)}) collective-permute-start(bf16[112,256]{1,0:T(8,128)(2,1)S(1)} %get-tuple-element.661), channel_id=1, source_target_pairs={{0,32},{16,48},{32,0},{48,16},{1,33},{17,49},{33,1},{49,17},{2,34}... | collective-permute-start | bytes 172040 | tf_op jit(solution)/shard_map/while/body/eval_jaxpr/ppermute | solution.py:16
  10.2 2.7 %collective-permute-start.4 = (bf16[112,256]{1,0:T(8,128)(2,1)S(1)}, bf16[112,256]{1,0:T(8,128)(2,1)S(1)}, u32[]{:S(2)}, u32[]{:S(2)}) collective-permute-start(bf16[112,256]{1,0:T(8,128)(2,1)S(1)} %get-tuple-element.661), channel_id=1, source_target_pairs={{0,48},{16,0},{32,16},{48,32},{1,49},{17,1},{33,17},{49,33},{2,50}... | collective-permute-start | bytes 172040 | tf_op jit(solution)/shard_map/while/body/eval_jaxpr/ppermute | solution.py:16
  13.0 3.0 %collective-permute-done.3 = bf16[112,256]{1,0:T(8,128)(2,1)S(1)} collective-permute-done((bf16[112,256]{1,0:T(8,128)(2,1)S(1)}, bf16[112,256]{1,0:T(8,128)(2,1)S(1)}, u32[]{:S(2)}, u32[]{:S(2)}) %collective-permute-start.3) | collective-permute-done | bytes 57376 | tf_op jit(solution)/shard_map/while/body/eval_jaxpr/ppermute | solution.py:16
  16.6 3.2 %collective-permute-start.5 = (bf16[4,112,256]{2,1,0:T(8,128)(2,1)S(1)}, bf16[4,112,256]{2,1,0:T(8,128)(2,1)S(1)}, u32[]{:S(2)}, u32[]{:S(2)}) collective-permute-start(bf16[4,112,256]{2,1,0:T(8,128)(2,1)S(1)} %bitcast_dynamic-update-slice_fusion.29), channel_id=1, source_target_pairs={{0,128},{64,192},{128,0},{192,64},{1,129},{65,193},{129,1},{193,65... | collective-permute-start | bytes 688136 | tf_op jit(solution)/shard_map/while/body/eval_jaxpr/ppermute | solution.py:16
  20.7 2.6 %collective-permute-start.7 = (bf16[4,112,256]{2,1,0:T(8,128)(2,1)S(1)}, bf16[4,112,256]{2,1,0:T(8,128)(2,1)S(1)}, u32[]{:S(2)}, u32[]{:S(2)}) collective-permute-start(bf16[4,112,256]{2,1,0:T(8,128)(2,1)S(1)} %bitcast_dynamic-update-slice_fusion.29), channel_id=1, source_target_pairs={{0,192},{64,0},{128,64},{192,128},{1,193},{65,1},{129,65},{193,129... | collective-permute-start | bytes 688136 | tf_op jit(solution)/shard_map/while/body/eval_jaxpr/ppermute | solution.py:16
  23.5 2.9 %collective-permute-start.10 = (bf16[4,112,256]{2,1,0:T(8,128)(2,1)S(1)}, bf16[4,112,256]{2,1,0:T(8,128)(2,1)S(1)}, u32[]{:S(2)}, u32[]{:S(2)}) collective-permute-start(bf16[4,112,256]{2,1,0:T(8,128)(2,1)S(1)} %collective-permute-done.8), channel_id=1, source_target_pairs={{0,192},{64,0},{128,64},{192,128},{1,193},{65,1},{129,65},{193,129... | collective-permute-start | bytes 688136 | tf_op jit(solution)/shard_map/while/body/eval_jaxpr/ppermute | solution.py:16
  31.7 2.3 %collective-permute-done.9 = bf16[4,112,256]{2,1,0:T(8,128)(2,1)S(1)} collective-permute-done((bf16[4,112,256]{2,1,0:T(8,128)(2,1)S(1)}, bf16[4,112,256]{2,1,0:T(8,128)(2,1)S(1)}, u32[]{:S(2)}, u32[]{:S(2)}) %collective-permute-start.9) | collective-permute-done | bytes 229408 | tf_op jit(solution)/shard_map/while/body/eval_jaxpr/ppermute | solution.py:16
  48.2 4.8 %collective-permute-start.2 = (bf16[112,256]{1,0:T(8,128)(2,1)S(1)}, bf16[112,256]{1,0:T(8,128)(2,1)S(1)}, u32[]{:S(2)}, u32[]{:S(2)}) collective-permute-start(bf16[112,256]{1,0:T(8,128)(2,1)S(1)} %get-tuple-element.661), channel_id=1, source_target_pairs={{0,32},{16,48},{32,0},{48,16},{1,33},{17,49},{33,1},{49,17},{2,34}... | collective-permute-start | bytes 172040 | tf_op jit(solution)/shard_map/while/body/eval_jaxpr/ppermute | solution.py:16
  54.6 2.5 %collective-permute-start.4 = (bf16[112,256]{1,0:T(8,128)(2,1)S(1)}, bf16[112,256]{1,0:T(8,128)(2,1)S(1)}, u32[]{:S(2)}, u32[]{:S(2)}) collective-permute-start(bf16[112,256]{1,0:T(8,128)(2,1)S(1)} %get-tuple-element.661), channel_id=1, source_target_pairs={{0,48},{16,0},{32,16},{48,32},{1,49},{17,1},{33,17},{49,33},{2,50}... | collective-permute-start | bytes 172040 | tf_op jit(solution)/shard_map/while/body/eval_jaxpr/ppermute | solution.py:16
  57.2 2.6 %collective-permute-done.3 = bf16[112,256]{1,0:T(8,128)(2,1)S(1)} collective-permute-done((bf16[112,256]{1,0:T(8,128)(2,1)S(1)}, bf16[112,256]{1,0:T(8,128)(2,1)S(1)}, u32[]{:S(2)}, u32[]{:S(2)}) %collective-permute-start.3) | collective-permute-done | bytes 57376 | tf_op jit(solution)/shard_map/while/body/eval_jaxpr/ppermute | solution.py:16
  60.4 2.4 %collective-permute-start.5 = (bf16[4,112,256]{2,1,0:T(8,128)(2,1)S(1)}, bf16[4,112,256]{2,1,0:T(8,128)(2,1)S(1)}, u32[]{:S(2)}, u32[]{:S(2)}) collective-permute-start(bf16[4,112,256]{2,1,0:T(8,128)(2,1)S(1)} %bitcast_dynamic-update-slice_fusion.29), channel_id=1, source_target_pairs={{0,128},{64,192},{128,0},{192,64},{1,129},{65,193},{129,1},{193,65... | collective-permute-start | bytes 688136 | tf_op jit(solution)/shard_map/while/body/eval_jaxpr/ppermute | solution.py:16
  75.7 2.5 %collective-permute-done.9 = bf16[4,112,256]{2,1,0:T(8,128)(2,1)S(1)} collective-permute-done((bf16[4,112,256]{2,1,0:T(8,128)(2,1)S(1)}, bf16[4,112,256]{2,1,0:T(8,128)(2,1)S(1)}, u32[]{:S(2)}, u32[]{:S(2)}) %collective-permute-start.9) | collective-permute-done | bytes 229408 | tf_op jit(solution)/shard_map/while/body/eval_jaxpr/ppermute | solution.py:16
  86.5 2.5 %collective-permute-done.15 = f32[104,256]{1,0:T(8,128)S(1)} collective-permute-done((f32[104,256]{1,0:T(8,128)S(1)}, f32[104,256]{1,0:T(8,128)S(1)}, u32[]{:S(2)}, u32[]{:S(2)}) %collective-permute-start.15) | collective-permute-done | bytes 106528 | tf_op jit(solution)/shard_map/while/body/eval_jaxpr/ppermute | solution.py:16
  92.5 3.5 %collective-permute-start.2 = (bf16[112,256]{1,0:T(8,128)(2,1)S(1)}, bf16[112,256]{1,0:T(8,128)(2,1)S(1)}, u32[]{:S(2)}, u32[]{:S(2)}) collective-permute-start(bf16[112,256]{1,0:T(8,128)(2,1)S(1)} %get-tuple-element.661), channel_id=1, source_target_pairs={{0,32},{16,48},{32,0},{48,16},{1,33},{17,49},{33,1},{49,17},{2,34}... | collective-permute-start | bytes 172040 | tf_op jit(solution)/shard_map/while/body/eval_jaxpr/ppermute | solution.py:16
  97.0 3.1 %collective-permute-start.4 = (bf16[112,256]{1,0:T(8,128)(2,1)S(1)}, bf16[112,256]{1,0:T(8,128)(2,1)S(1)}, u32[]{:S(2)}, u32[]{:S(2)}) collective-permute-start(bf16[112,256]{1,0:T(8,128)(2,1)S(1)} %get-tuple-element.661), channel_id=1, source_target_pairs={{0,48},{16,0},{32,16},{48,32},{1,49},{17,1},{33,17},{49,33},{2,50}... | collective-permute-start | bytes 172040 | tf_op jit(solution)/shard_map/while/body/eval_jaxpr/ppermute | solution.py:16
  110.4 2.9 %collective-permute-start.10 = (bf16[4,112,256]{2,1,0:T(8,128)(2,1)S(1)}, bf16[4,112,256]{2,1,0:T(8,128)(2,1)S(1)}, u32[]{:S(2)}, u32[]{:S(2)}) collective-permute-start(bf16[4,112,256]{2,1,0:T(8,128)(2,1)S(1)} %collective-permute-done.8), channel_id=1, source_target_pairs={{0,192},{64,0},{128,64},{192,128},{1,193},{65,1},{129,65},{193,129... | collective-permute-start | bytes 688136 | tf_op jit(solution)/shard_map/while/body/eval_jaxpr/ppermute | solution.py:16
  115.2 2.7 %collective-permute-done.6 = bf16[4,112,256]{2,1,0:T(8,128)(2,1)S(1)} collective-permute-done((bf16[4,112,256]{2,1,0:T(8,128)(2,1)S(1)}, bf16[4,112,256]{2,1,0:T(8,128)(2,1)S(1)}, u32[]{:S(2)}, u32[]{:S(2)}) %collective-permute-start.6) | collective-permute-done | bytes 229408 | tf_op jit(solution)/shard_map/while/body/eval_jaxpr/ppermute | solution.py:16
  119.0 2.4 %collective-permute-done.9 = bf16[4,112,256]{2,1,0:T(8,128)(2,1)S(1)} collective-permute-done((bf16[4,112,256]{2,1,0:T(8,128)(2,1)S(1)}, bf16[4,112,256]{2,1,0:T(8,128)(2,1)S(1)}, u32[]{:S(2)}, u32[]{:S(2)}) %collective-permute-start.9) | collective-permute-done | bytes 229408 | tf_op jit(solution)/shard_map/while/body/eval_jaxpr/ppermute | solution.py:16
  126.0 3.1 %collective-permute-start.16 = (f32[104,256]{1,0:T(8,128)S(1)}, f32[104,256]{1,0:T(8,128)S(1)}, u32[]{:S(2)}, u32[]{:S(2)}) collective-permute-start(f32[104,256]{1,0:T(8,128)S(1)} %get-tuple-element.629), channel_id=1, source_target_pairs={{0,6},{2,0},{4,2},{6,4},{1,7},{3,1},{5,3},{7,5},{8,14},{10,8},{12,... | collective-permute-start | bytes 319496 | tf_op jit(solution)/shard_map/while/body/eval_jaxpr/ppermute | solution.py:16
  129.6 2.5 %collective-permute-done.15 = f32[104,256]{1,0:T(8,128)S(1)} collective-permute-done((f32[104,256]{1,0:T(8,128)S(1)}, f32[104,256]{1,0:T(8,128)S(1)}, u32[]{:S(2)}, u32[]{:S(2)}) %collective-permute-start.15) | collective-permute-done | bytes 106528 | tf_op jit(solution)/shard_map/while/body/eval_jaxpr/ppermute | solution.py:16
  137.1 13.3 %all_to_all.45 = f32[16,8,256]{2,1,0:T(8,128)S(1)} all-to-all(f32[16,8,256]{2,1,0:T(8,128)S(1)} %broadcast_in_dim.298), channel_id=1, replica_groups=mesh['y'=4,'zs'=4,'zp'=2,'x'=4,'core'=2] {'y','x'}, dimensions={0} | all-to-all | bytes 262144 | tf_op jit(solution)/shard_map/all_to_all | solution.py:12
  151.0 5.3 %all-to-all-start.8 = ((f32[8,8,256]{2,1,0:T(8,128)}), f32[8,8,256]{2,1,0:T(8,128)S(1)}, u32[]{:S(2)}, u32[]{:S(2)}) async-start(f32[8,8,256]{2,1,0:T(8,128)} %broadcast_in_dim.299), calls=%async_computation.8 | async-start | bytes 131072 | tf_op jit(solution)/shard_map/all_to_all | solution.py:12
  156.4 6.8 %all-to-all-done.8 = f32[8,8,256]{2,1,0:T(8,128)S(1)} async-done(((f32[8,8,256]{2,1,0:T(8,128)}), f32[8,8,256]{2,1,0:T(8,128)S(1)}, u32[]{:S(2)}, u32[]{:S(2)}) %all-to-all-start.8) | async-done | bytes 65568 | tf_op jit(solution)/shard_map/all_to_all | solution.py:12
  (210 shorter events, 76.9 us)
Async XLA Ops:
  2.4 10.6 %collective-permute-start.2 = (bf16[112,256]{1,0:T(8,128)(2,1)S(1)}, bf16[112,256]{1,0:T(8,128)(2,1)S(1)}, u32[]{:S(2)}, u32[]{:S(2)}) collective-permute-start(bf16[112,256]{1,0:T(8,128)(2,1)S(1)} %get-tuple-element.661), channel_id=1, source_target_pairs={{0,32},{16,48},{32,0},{48,16},{1,33},{17,49},{33,1},{49,17},{2,34}... | collective-permute-start | bytes 172040 | tf_op jit(solution)/shard_map/while/body/eval_jaxpr/ppermute | solution.py:16
  8.8 7.3 %collective-permute-start.3 = (bf16[112,256]{1,0:T(8,128)(2,1)S(1)}, bf16[112,256]{1,0:T(8,128)(2,1)S(1)}, u32[]{:S(2)}, u32[]{:S(2)}) collective-permute-start(bf16[112,256]{1,0:T(8,128)(2,1)S(1)} %get-tuple-element.661), channel_id=1, source_target_pairs={{0,16},{16,32},{32,48},{48,0},{1,17},{17,33},{33,49},{49,1},{2,18}... | collective-permute-start | bytes 172040 | tf_op jit(solution)/shard_map/while/body/eval_jaxpr/ppermute | solution.py:16
  16.6 10.0 %collective-permute-start.5 = (bf16[4,112,256]{2,1,0:T(8,128)(2,1)S(1)}, bf16[4,112,256]{2,1,0:T(8,128)(2,1)S(1)}, u32[]{:S(2)}, u32[]{:S(2)}) collective-permute-start(bf16[4,112,256]{2,1,0:T(8,128)(2,1)S(1)} %bitcast_dynamic-update-slice_fusion.29), channel_id=1, source_target_pairs={{0,128},{64,192},{128,0},{192,64},{1,129},{65,193},{129,1},{193,65... | collective-permute-start | bytes 688136 | tf_op jit(solution)/shard_map/while/body/eval_jaxpr/ppermute | solution.py:16
  19.9 10.8 %collective-permute-start.6 = (bf16[4,112,256]{2,1,0:T(8,128)(2,1)S(1)}, bf16[4,112,256]{2,1,0:T(8,128)(2,1)S(1)}, u32[]{:S(2)}, u32[]{:S(2)}) collective-permute-start(bf16[4,112,256]{2,1,0:T(8,128)(2,1)S(1)} %bitcast_dynamic-update-slice_fusion.29), channel_id=1, source_target_pairs={{0,64},{64,128},{128,192},{192,0},{1,65},{65,129},{129,193},{193,1... | collective-permute-start | bytes 688136 | tf_op jit(solution)/shard_map/while/body/eval_jaxpr/ppermute | solution.py:16
  20.7 11.0 %collective-permute-start.7 = (bf16[4,112,256]{2,1,0:T(8,128)(2,1)S(1)}, bf16[4,112,256]{2,1,0:T(8,128)(2,1)S(1)}, u32[]{:S(2)}, u32[]{:S(2)}) collective-permute-start(bf16[4,112,256]{2,1,0:T(8,128)(2,1)S(1)} %bitcast_dynamic-update-slice_fusion.29), channel_id=1, source_target_pairs={{0,192},{64,0},{128,64},{192,128},{1,193},{65,1},{129,65},{193,129... | collective-permute-start | bytes 688136 | tf_op jit(solution)/shard_map/while/body/eval_jaxpr/ppermute | solution.py:16
  23.2 10.9 %collective-permute-start.9 = (bf16[4,112,256]{2,1,0:T(8,128)(2,1)S(1)}, bf16[4,112,256]{2,1,0:T(8,128)(2,1)S(1)}, u32[]{:S(2)}, u32[]{:S(2)}) collective-permute-start(bf16[4,112,256]{2,1,0:T(8,128)(2,1)S(1)} %collective-permute-done.8), channel_id=1, source_target_pairs={{0,64},{64,128},{128,192},{192,0},{1,65},{65,129},{129,193},{193,1... | collective-permute-start | bytes 688136 | tf_op jit(solution)/shard_map/while/body/eval_jaxpr/ppermute | solution.py:16
  23.5 10.6 %collective-permute-start.10 = (bf16[4,112,256]{2,1,0:T(8,128)(2,1)S(1)}, bf16[4,112,256]{2,1,0:T(8,128)(2,1)S(1)}, u32[]{:S(2)}, u32[]{:S(2)}) collective-permute-start(bf16[4,112,256]{2,1,0:T(8,128)(2,1)S(1)} %collective-permute-done.8), channel_id=1, source_target_pairs={{0,192},{64,0},{128,64},{192,128},{1,193},{65,1},{129,65},{193,129... | collective-permute-start | bytes 688136 | tf_op jit(solution)/shard_map/while/body/eval_jaxpr/ppermute | solution.py:16
  26.6 7.5 %collective-permute-start.11 = (bf16[4,112,256]{2,1,0:T(8,128)(2,1)S(1)}, bf16[4,112,256]{2,1,0:T(8,128)(2,1)S(1)}, u32[]{:S(2)}, u32[]{:S(2)}) collective-permute-start(bf16[4,112,256]{2,1,0:T(8,128)(2,1)S(1)} %collective-permute-done.5), channel_id=1, source_target_pairs={{0,8},{8,0},{1,9},{9,1},{2,10},{10,2},{3,11},{11,3},{4,12},{12,4},... | collective-permute-start | bytes 688136 | tf_op jit(solution)/shard_map/while/body/eval_jaxpr/ppermute | solution.py:35
  48.2 9.0 %collective-permute-start.2 = (bf16[112,256]{1,0:T(8,128)(2,1)S(1)}, bf16[112,256]{1,0:T(8,128)(2,1)S(1)}, u32[]{:S(2)}, u32[]{:S(2)}) collective-permute-start(bf16[112,256]{1,0:T(8,128)(2,1)S(1)} %get-tuple-element.661), channel_id=1, source_target_pairs={{0,32},{16,48},{32,0},{48,16},{1,33},{17,49},{33,1},{49,17},{2,34}... | collective-permute-start | bytes 172040 | tf_op jit(solution)/shard_map/while/body/eval_jaxpr/ppermute | solution.py:16
  60.4 10.1 %collective-permute-start.5 = (bf16[4,112,256]{2,1,0:T(8,128)(2,1)S(1)}, bf16[4,112,256]{2,1,0:T(8,128)(2,1)S(1)}, u32[]{:S(2)}, u32[]{:S(2)}) collective-permute-start(bf16[4,112,256]{2,1,0:T(8,128)(2,1)S(1)} %bitcast_dynamic-update-slice_fusion.29), channel_id=1, source_target_pairs={{0,128},{64,192},{128,0},{192,64},{1,129},{65,193},{129,1},{193,65... | collective-permute-start | bytes 688136 | tf_op jit(solution)/shard_map/while/body/eval_jaxpr/ppermute | solution.py:16
  62.9 11.2 %collective-permute-start.6 = (bf16[4,112,256]{2,1,0:T(8,128)(2,1)S(1)}, bf16[4,112,256]{2,1,0:T(8,128)(2,1)S(1)}, u32[]{:S(2)}, u32[]{:S(2)}) collective-permute-start(bf16[4,112,256]{2,1,0:T(8,128)(2,1)S(1)} %bitcast_dynamic-update-slice_fusion.29), channel_id=1, source_target_pairs={{0,64},{64,128},{128,192},{192,0},{1,65},{65,129},{129,193},{193,1... | collective-permute-start | bytes 688136 | tf_op jit(solution)/shard_map/while/body/eval_jaxpr/ppermute | solution.py:16
  64.4 11.2 %collective-permute-start.7 = (bf16[4,112,256]{2,1,0:T(8,128)(2,1)S(1)}, bf16[4,112,256]{2,1,0:T(8,128)(2,1)S(1)}, u32[]{:S(2)}, u32[]{:S(2)}) collective-permute-start(bf16[4,112,256]{2,1,0:T(8,128)(2,1)S(1)} %bitcast_dynamic-update-slice_fusion.29), channel_id=1, source_target_pairs={{0,192},{64,0},{128,64},{192,128},{1,193},{65,1},{129,65},{193,129... | collective-permute-start | bytes 688136 | tf_op jit(solution)/shard_map/while/body/eval_jaxpr/ppermute | solution.py:16
  66.4 11.7 %collective-permute-start.9 = (bf16[4,112,256]{2,1,0:T(8,128)(2,1)S(1)}, bf16[4,112,256]{2,1,0:T(8,128)(2,1)S(1)}, u32[]{:S(2)}, u32[]{:S(2)}) collective-permute-start(bf16[4,112,256]{2,1,0:T(8,128)(2,1)S(1)} %collective-permute-done.8), channel_id=1, source_target_pairs={{0,64},{64,128},{128,192},{192,0},{1,65},{65,129},{129,193},{193,1... | collective-permute-start | bytes 688136 | tf_op jit(solution)/shard_map/while/body/eval_jaxpr/ppermute | solution.py:16
  68.0 10.4 %collective-permute-start.10 = (bf16[4,112,256]{2,1,0:T(8,128)(2,1)S(1)}, bf16[4,112,256]{2,1,0:T(8,128)(2,1)S(1)}, u32[]{:S(2)}, u32[]{:S(2)}) collective-permute-start(bf16[4,112,256]{2,1,0:T(8,128)(2,1)S(1)} %collective-permute-done.8), channel_id=1, source_target_pairs={{0,192},{64,0},{128,64},{192,128},{1,193},{65,1},{129,65},{193,129... | collective-permute-start | bytes 688136 | tf_op jit(solution)/shard_map/while/body/eval_jaxpr/ppermute | solution.py:16
  70.6 7.9 %collective-permute-start.11 = (bf16[4,112,256]{2,1,0:T(8,128)(2,1)S(1)}, bf16[4,112,256]{2,1,0:T(8,128)(2,1)S(1)}, u32[]{:S(2)}, u32[]{:S(2)}) collective-permute-start(bf16[4,112,256]{2,1,0:T(8,128)(2,1)S(1)} %collective-permute-done.5), channel_id=1, source_target_pairs={{0,8},{8,0},{1,9},{9,1},{2,10},{10,2},{3,11},{11,3},{4,12},{12,4},... | collective-permute-start | bytes 688136 | tf_op jit(solution)/shard_map/while/body/eval_jaxpr/ppermute | solution.py:35
  92.5 8.2 %collective-permute-start.2 = (bf16[112,256]{1,0:T(8,128)(2,1)S(1)}, bf16[112,256]{1,0:T(8,128)(2,1)S(1)}, u32[]{:S(2)}, u32[]{:S(2)}) collective-permute-start(bf16[112,256]{1,0:T(8,128)(2,1)S(1)} %get-tuple-element.661), channel_id=1, source_target_pairs={{0,32},{16,48},{32,0},{48,16},{1,33},{17,49},{33,1},{49,17},{2,34}... | collective-permute-start | bytes 172040 | tf_op jit(solution)/shard_map/while/body/eval_jaxpr/ppermute | solution.py:16
  102.9 7.2 %collective-permute-start.8 = (bf16[4,112,256]{2,1,0:T(8,128)(2,1)S(1)}, bf16[4,112,256]{2,1,0:T(8,128)(2,1)S(1)}, u32[]{:S(2)}, u32[]{:S(2)}) collective-permute-start(bf16[4,112,256]{2,1,0:T(8,128)(2,1)S(1)} %bitcast_dynamic-update-slice_fusion.29), channel_id=1, source_target_pairs={{0,8},{8,0},{1,9},{9,1},{2,10},{10,2},{3,11},{11,3},{4,12},{12,4},... | collective-permute-start | bytes 688136 | tf_op jit(solution)/shard_map/while/body/eval_jaxpr/ppermute | solution.py:33
  104.3 10.0 %collective-permute-start.5 = (bf16[4,112,256]{2,1,0:T(8,128)(2,1)S(1)}, bf16[4,112,256]{2,1,0:T(8,128)(2,1)S(1)}, u32[]{:S(2)}, u32[]{:S(2)}) collective-permute-start(bf16[4,112,256]{2,1,0:T(8,128)(2,1)S(1)} %bitcast_dynamic-update-slice_fusion.29), channel_id=1, source_target_pairs={{0,128},{64,192},{128,0},{192,64},{1,129},{65,193},{129,1},{193,65... | collective-permute-start | bytes 688136 | tf_op jit(solution)/shard_map/while/body/eval_jaxpr/ppermute | solution.py:16
  106.8 11.2 %collective-permute-start.6 = (bf16[4,112,256]{2,1,0:T(8,128)(2,1)S(1)}, bf16[4,112,256]{2,1,0:T(8,128)(2,1)S(1)}, u32[]{:S(2)}, u32[]{:S(2)}) collective-permute-start(bf16[4,112,256]{2,1,0:T(8,128)(2,1)S(1)} %bitcast_dynamic-update-slice_fusion.29), channel_id=1, source_target_pairs={{0,64},{64,128},{128,192},{192,0},{1,65},{65,129},{129,193},{193,1... | collective-permute-start | bytes 688136 | tf_op jit(solution)/shard_map/while/body/eval_jaxpr/ppermute | solution.py:16
  108.1 10.8 %collective-permute-start.7 = (bf16[4,112,256]{2,1,0:T(8,128)(2,1)S(1)}, bf16[4,112,256]{2,1,0:T(8,128)(2,1)S(1)}, u32[]{:S(2)}, u32[]{:S(2)}) collective-permute-start(bf16[4,112,256]{2,1,0:T(8,128)(2,1)S(1)} %bitcast_dynamic-update-slice_fusion.29), channel_id=1, source_target_pairs={{0,192},{64,0},{128,64},{192,128},{1,193},{65,1},{129,65},{193,129... | collective-permute-start | bytes 688136 | tf_op jit(solution)/shard_map/while/body/eval_jaxpr/ppermute | solution.py:16
  110.1 11.3 %collective-permute-start.9 = (bf16[4,112,256]{2,1,0:T(8,128)(2,1)S(1)}, bf16[4,112,256]{2,1,0:T(8,128)(2,1)S(1)}, u32[]{:S(2)}, u32[]{:S(2)}) collective-permute-start(bf16[4,112,256]{2,1,0:T(8,128)(2,1)S(1)} %collective-permute-done.8), channel_id=1, source_target_pairs={{0,64},{64,128},{128,192},{192,0},{1,65},{65,129},{129,193},{193,1... | collective-permute-start | bytes 688136 | tf_op jit(solution)/shard_map/while/body/eval_jaxpr/ppermute | solution.py:16
  110.4 11.0 %collective-permute-start.10 = (bf16[4,112,256]{2,1,0:T(8,128)(2,1)S(1)}, bf16[4,112,256]{2,1,0:T(8,128)(2,1)S(1)}, u32[]{:S(2)}, u32[]{:S(2)}) collective-permute-start(bf16[4,112,256]{2,1,0:T(8,128)(2,1)S(1)} %collective-permute-done.8), channel_id=1, source_target_pairs={{0,192},{64,0},{128,64},{192,128},{1,193},{65,1},{129,65},{193,129... | collective-permute-start | bytes 688136 | tf_op jit(solution)/shard_map/while/body/eval_jaxpr/ppermute | solution.py:16
  126.0 7.6 %collective-permute-start.16 = (f32[104,256]{1,0:T(8,128)S(1)}, f32[104,256]{1,0:T(8,128)S(1)}, u32[]{:S(2)}, u32[]{:S(2)}) collective-permute-start(f32[104,256]{1,0:T(8,128)S(1)} %get-tuple-element.629), channel_id=1, source_target_pairs={{0,6},{2,0},{4,2},{6,4},{1,7},{3,1},{5,3},{7,5},{8,14},{10,8},{12,... | collective-permute-start | bytes 319496 | tf_op jit(solution)/shard_map/while/body/eval_jaxpr/ppermute | solution.py:16
  151.0 12.2 %all-to-all-start.8 = ((f32[8,8,256]{2,1,0:T(8,128)}), f32[8,8,256]{2,1,0:T(8,128)S(1)}, u32[]{:S(2)}, u32[]{:S(2)}) async-start(f32[8,8,256]{2,1,0:T(8,128)} %broadcast_in_dim.299), calls=%async_computation.8 | async-start | bytes 131072 | tf_op jit(solution)/shard_map/all_to_all | solution.py:12
  (34 other events, 182.7 us)

commit v3 on v2

--- a/solution.py
+++ b/solution.py
@@ -137,10 +137,9 @@
     error_sq = ROUNDING**2 * jnp.sum(step_1 * step_1 * (g11 / g00) * spread_sq)
     close = error_sq < ALLOWED**2 * jnp.sum(last_sq)
 
-    def short():
-        direction = ahead * v0 - step_0 * v1
-        image = ahead * v1 - step_0 * v2
-        return (kept * dense + step_0 * v0 + step_1 * direction, residual - step_1 * image)
+    direction = ahead * v0 - step_0 * v1
+    image = ahead * v1 - step_0 * v2
+    short = (kept * dense + step_0 * v0 + step_1 * direction, residual - step_1 * image)
 
     def long():
         fresh = total_sums([(residual, residual)])[0]
@@ -150,7 +149,7 @@
         step = fresh / total_sums([(direction, image)])[0]
         return (kept * dense + step_0 * v0 + step * direction, residual - step * image)
 
-    return lax.cond(close, short, long)
+    return lax.cond(close, lambda: short, long)
 
 
 def solution(mesh):

time: 167 us -> 167 us (level)
  no operation moved by 1% of the time
where the time goes in v3:
time: 167 us; the launch traced here: 166 us
  starting transfers between devices  81.4 us (49%)
  waiting for transfers between devices  54.3 us (33%)
  blocking collectives  13.3 us (8%)
  matrix products  5.91 us (4%)
  other arithmetic  5.37 us (3%)
  local copies, waits for them, and re-layouts  2.57 us (2%)
  between operations  2.09 us (1%)
    ppermute x33, starting transfers between devices, moved(): lax.ppermute(block, axis, [(i, (i + shift) % size) for i in range(size)])  66.5 us
    ppermute x33, waiting for transfers between devices, moved(): lax.ppermute(block, axis, [(i, (i + shift) % size) for i in range(size)])  43.7 us
    all_to_all x1, blocking collectives, spread(): lax.all_to_all(jnp.broadcast_to(block[None], (size,) + block.shape), axes...  13.3 us
    all_to_all x1, waiting for transfers between devices, spread(): lax.all_to_all(jnp.broadcast_to(block[None], (size,) + block.shape), axes...  6.84 us
    dot_general x3, matrix products, product(): jnp.einsum('cst,tk->csk', hessian, gathered, preferred_element_type=F32)  5.91 us
    all_to_all x1, starting transfers between devices, spread(): lax.all_to_all(jnp.broadcast_to(block[None], (size,) + block.shape), axes...  5.32 us
    ppermute x3, starting transfers between devices, gather_rows(): other[2] = lax.ppermute(mine[2], 'zp', swap)  4.02 us
  transfers between devices with their start and end apart: 53, of which 39 were waited for; matrix products, arithmetic and copies ran while one was open for 1% of the time, Pallas kernels for 0%

profile of v3, /device:TPU:32, one launch (start us, length us, event | category | flops | bytes accessed | tf_op | source)
XLA Modules:
  0.0 166.1 jit_solution(2340567776308202267)
XLA Ops:
  2.4 133.3 %while.25 = (s32[]{:T(128)}, bf16[112,256]{1,0:T(8,128)(2,1)S(1)}, f32[3,104,256]{2,1,0:T(8,128)S(1)}, f32[8,104,256]{2,1,0:T(8,128)S(1)}, f32[256]{0:T(256)S(1)...) while((s32[]{:T(128)}, bf16[112,256]{1,0:T(8,128)(2,1)S(1)}, ...), condition=%wide.region_5.6_spmd.clone, body=%wide.region_0.5_spmd.clone.sunk | while | flops 1420384896 | bytes 55856980 | solution.py:119
  2.4 6.4 %collective-permute-start.2 = (bf16[112,256]{1,0:T(8,128)(2,1)S(1)}, bf16[112,256]{1,0:T(8,128)(2,1)S(1)}, u32[]{:S(2)}, u32[]{:S(2)}) collective-permute-start(bf16[112,256]{1,0:T(8,128)(2,1)S(1)} %get-tuple-element.721), channel_id=1, source_target_pairs={{0,32},{16,48},{32,0},{48,16},{1,33},{17,49},{33,1},{49,17},{2,34}... | collective-permute-start | bytes 172040 | tf_op jit(solution)/shard_map/while/body/eval_jaxpr/ppermute | solution.py:16
  10.2 2.7 %collective-permute-start.4 = (bf16[112,256]{1,0:T(8,128)(2,1)S(1)}, bf16[112,256]{1,0:T(8,128)(2,1)S(1)}, u32[]{:S(2)}, u32[]{:S(2)}) collective-permute-start(bf16[112,256]{1,0:T(8,128)(2,1)S(1)} %get-tuple-element.721), channel_id=1, source_target_pairs={{0,48},{16,0},{32,16},{48,32},{1,49},{17,1},{33,17},{49,33},{2,50}... | collective-permute-start | bytes 172040 | tf_op jit(solution)/shard_map/while/body/eval_jaxpr/ppermute | solution.py:16
  13.0 3.0 %collective-permute-done.3 = bf16[112,256]{1,0:T(8,128)(2,1)S(1)} collective-permute-done((bf16[112,256]{1,0:T(8,128)(2,1)S(1)}, bf16[112,256]{1,0:T(8,128)(2,1)S(1)}, u32[]{:S(2)}, u32[]{:S(2)}) %collective-permute-start.3) | collective-permute-done | bytes 57376 | tf_op jit(solution)/shard_map/while/body/eval_jaxpr/ppermute | solution.py:16
  16.6 3.2 %collective-permute-start.5 = (bf16[4,112,256]{2,1,0:T(8,128)(2,1)S(1)}, bf16[4,112,256]{2,1,0:T(8,128)(2,1)S(1)}, u32[]{:S(2)}, u32[]{:S(2)}) collective-permute-start(bf16[4,112,256]{2,1,0:T(8,128)(2,1)S(1)} %bitcast_dynamic-update-slice_fusion.29), channel_id=1, source_target_pairs={{0,128},{64,192},{128,0},{192,64},{1,129},{65,193},{129,1},{193,65... | collective-permute-start | bytes 688136 | tf_op jit(solution)/shard_map/while/body/eval_jaxpr/ppermute | solution.py:16
  20.7 2.6 %collective-permute-start.7 = (bf16[4,112,256]{2,1,0:T(8,128)(2,1)S(1)}, bf16[4,112,256]{2,1,0:T(8,128)(2,1)S(1)}, u32[]{:S(2)}, u32[]{:S(2)}) collective-permute-start(bf16[4,112,256]{2,1,0:T(8,128)(2,1)S(1)} %bitcast_dynamic-update-slice_fusion.29), channel_id=1, source_target_pairs={{0,192},{64,0},{128,64},{192,128},{1,193},{65,1},{129,65},{193,129... | collective-permute-start | bytes 688136 | tf_op jit(solution)/shard_map/while/body/eval_jaxpr/ppermute | solution.py:16
  23.5 2.9 %collective-permute-start.10 = (bf16[4,112,256]{2,1,0:T(8,128)(2,1)S(1)}, bf16[4,112,256]{2,1,0:T(8,128)(2,1)S(1)}, u32[]{:S(2)}, u32[]{:S(2)}) collective-permute-start(bf16[4,112,256]{2,1,0:T(8,128)(2,1)S(1)} %collective-permute-done.8), channel_id=1, source_target_pairs={{0,192},{64,0},{128,64},{192,128},{1,193},{65,1},{129,65},{193,129... | collective-permute-start | bytes 688136 | tf_op jit(solution)/shard_map/while/body/eval_jaxpr/ppermute | solution.py:16
  31.7 2.3 %collective-permute-done.9 = bf16[4,112,256]{2,1,0:T(8,128)(2,1)S(1)} collective-permute-done((bf16[4,112,256]{2,1,0:T(8,128)(2,1)S(1)}, bf16[4,112,256]{2,1,0:T(8,128)(2,1)S(1)}, u32[]{:S(2)}, u32[]{:S(2)}) %collective-permute-start.9) | collective-permute-done | bytes 229408 | tf_op jit(solution)/shard_map/while/body/eval_jaxpr/ppermute | solution.py:16
  48.2 4.8 %collective-permute-start.2 = (bf16[112,256]{1,0:T(8,128)(2,1)S(1)}, bf16[112,256]{1,0:T(8,128)(2,1)S(1)}, u32[]{:S(2)}, u32[]{:S(2)}) collective-permute-start(bf16[112,256]{1,0:T(8,128)(2,1)S(1)} %get-tuple-element.721), channel_id=1, source_target_pairs={{0,32},{16,48},{32,0},{48,16},{1,33},{17,49},{33,1},{49,17},{2,34}... | collective-permute-start | bytes 172040 | tf_op jit(solution)/shard_map/while/body/eval_jaxpr/ppermute | solution.py:16
  54.6 2.5 %collective-permute-start.4 = (bf16[112,256]{1,0:T(8,128)(2,1)S(1)}, bf16[112,256]{1,0:T(8,128)(2,1)S(1)}, u32[]{:S(2)}, u32[]{:S(2)}) collective-permute-start(bf16[112,256]{1,0:T(8,128)(2,1)S(1)} %get-tuple-element.721), channel_id=1, source_target_pairs={{0,48},{16,0},{32,16},{48,32},{1,49},{17,1},{33,17},{49,33},{2,50}... | collective-permute-start | bytes 172040 | tf_op jit(solution)/shard_map/while/body/eval_jaxpr/ppermute | solution.py:16
  57.2 2.6 %collective-permute-done.3 = bf16[112,256]{1,0:T(8,128)(2,1)S(1)} collective-permute-done((bf16[112,256]{1,0:T(8,128)(2,1)S(1)}, bf16[112,256]{1,0:T(8,128)(2,1)S(1)}, u32[]{:S(2)}, u32[]{:S(2)}) %collective-permute-start.3) | collective-permute-done | bytes 57376 | tf_op jit(solution)/shard_map/while/body/eval_jaxpr/ppermute | solution.py:16
  60.4 2.4 %collective-permute-start.5 = (bf16[4,112,256]{2,1,0:T(8,128)(2,1)S(1)}, bf16[4,112,256]{2,1,0:T(8,128)(2,1)S(1)}, u32[]{:S(2)}, u32[]{:S(2)}) collective-permute-start(bf16[4,112,256]{2,1,0:T(8,128)(2,1)S(1)} %bitcast_dynamic-update-slice_fusion.29), channel_id=1, source_target_pairs={{0,128},{64,192},{128,0},{192,64},{1,129},{65,193},{129,1},{193,65... | collective-permute-start | bytes 688136 | tf_op jit(solution)/shard_map/while/body/eval_jaxpr/ppermute | solution.py:16
  75.7 2.5 %collective-permute-done.9 = bf16[4,112,256]{2,1,0:T(8,128)(2,1)S(1)} collective-permute-done((bf16[4,112,256]{2,1,0:T(8,128)(2,1)S(1)}, bf16[4,112,256]{2,1,0:T(8,128)(2,1)S(1)}, u32[]{:S(2)}, u32[]{:S(2)}) %collective-permute-start.9) | collective-permute-done | bytes 229408 | tf_op jit(solution)/shard_map/while/body/eval_jaxpr/ppermute | solution.py:16
  86.5 2.5 %collective-permute-done.15 = f32[104,256]{1,0:T(8,128)S(1)} collective-permute-done((f32[104,256]{1,0:T(8,128)S(1)}, f32[104,256]{1,0:T(8,128)S(1)}, u32[]{:S(2)}, u32[]{:S(2)}) %collective-permute-start.15) | collective-permute-done | bytes 106528 | tf_op jit(solution)/shard_map/while/body/eval_jaxpr/ppermute | solution.py:16
  92.5 3.5 %collective-permute-start.2 = (bf16[112,256]{1,0:T(8,128)(2,1)S(1)}, bf16[112,256]{1,0:T(8,128)(2,1)S(1)}, u32[]{:S(2)}, u32[]{:S(2)}) collective-permute-start(bf16[112,256]{1,0:T(8,128)(2,1)S(1)} %get-tuple-element.721), channel_id=1, source_target_pairs={{0,32},{16,48},{32,0},{48,16},{1,33},{17,49},{33,1},{49,17},{2,34}... | collective-permute-start | bytes 172040 | tf_op jit(solution)/shard_map/while/body/eval_jaxpr/ppermute | solution.py:16
  97.0 3.1 %collective-permute-start.4 = (bf16[112,256]{1,0:T(8,128)(2,1)S(1)}, bf16[112,256]{1,0:T(8,128)(2,1)S(1)}, u32[]{:S(2)}, u32[]{:S(2)}) collective-permute-start(bf16[112,256]{1,0:T(8,128)(2,1)S(1)} %get-tuple-element.721), channel_id=1, source_target_pairs={{0,48},{16,0},{32,16},{48,32},{1,49},{17,1},{33,17},{49,33},{2,50}... | collective-permute-start | bytes 172040 | tf_op jit(solution)/shard_map/while/body/eval_jaxpr/ppermute | solution.py:16
  110.4 2.9 %collective-permute-start.10 = (bf16[4,112,256]{2,1,0:T(8,128)(2,1)S(1)}, bf16[4,112,256]{2,1,0:T(8,128)(2,1)S(1)}, u32[]{:S(2)}, u32[]{:S(2)}) collective-permute-start(bf16[4,112,256]{2,1,0:T(8,128)(2,1)S(1)} %collective-permute-done.8), channel_id=1, source_target_pairs={{0,192},{64,0},{128,64},{192,128},{1,193},{65,1},{129,65},{193,129... | collective-permute-start | bytes 688136 | tf_op jit(solution)/shard_map/while/body/eval_jaxpr/ppermute | solution.py:16
  115.2 2.7 %collective-permute-done.6 = bf16[4,112,256]{2,1,0:T(8,128)(2,1)S(1)} collective-permute-done((bf16[4,112,256]{2,1,0:T(8,128)(2,1)S(1)}, bf16[4,112,256]{2,1,0:T(8,128)(2,1)S(1)}, u32[]{:S(2)}, u32[]{:S(2)}) %collective-permute-start.6) | collective-permute-done | bytes 229408 | tf_op jit(solution)/shard_map/while/body/eval_jaxpr/ppermute | solution.py:16
  119.0 2.4 %collective-permute-done.9 = bf16[4,112,256]{2,1,0:T(8,128)(2,1)S(1)} collective-permute-done((bf16[4,112,256]{2,1,0:T(8,128)(2,1)S(1)}, bf16[4,112,256]{2,1,0:T(8,128)(2,1)S(1)}, u32[]{:S(2)}, u32[]{:S(2)}) %collective-permute-start.9) | collective-permute-done | bytes 229408 | tf_op jit(solution)/shard_map/while/body/eval_jaxpr/ppermute | solution.py:16
  126.0 3.1 %collective-permute-start.16 = (f32[104,256]{1,0:T(8,128)S(1)}, f32[104,256]{1,0:T(8,128)S(1)}, u32[]{:S(2)}, u32[]{:S(2)}) collective-permute-start(f32[104,256]{1,0:T(8,128)S(1)} %get-tuple-element.689), channel_id=1, source_target_pairs={{0,6},{2,0},{4,2},{6,4},{1,7},{3,1},{5,3},{7,5},{8,14},{10,8},{12,... | collective-permute-start | bytes 319496 | tf_op jit(solution)/shard_map/while/body/eval_jaxpr/ppermute | solution.py:16
  129.6 2.5 %collective-permute-done.15 = f32[104,256]{1,0:T(8,128)S(1)} collective-permute-done((f32[104,256]{1,0:T(8,128)S(1)}, f32[104,256]{1,0:T(8,128)S(1)}, u32[]{:S(2)}, u32[]{:S(2)}) %collective-permute-start.15) | collective-permute-done | bytes 106528 | tf_op jit(solution)/shard_map/while/body/eval_jaxpr/ppermute | solution.py:16
  137.1 13.3 %all_to_all.45 = f32[16,8,256]{2,1,0:T(8,128)S(1)} all-to-all(f32[16,8,256]{2,1,0:T(8,128)S(1)} %broadcast_in_dim.298), channel_id=1, replica_groups=mesh['y'=4,'zs'=4,'zp'=2,'x'=4,'core'=2] {'y','x'}, dimensions={0} | all-to-all | bytes 262144 | tf_op jit(solution)/shard_map/all_to_all | solution.py:12
  151.0 5.3 %all-to-all-start.8 = ((f32[8,8,256]{2,1,0:T(8,128)}), f32[8,8,256]{2,1,0:T(8,128)S(1)}, u32[]{:S(2)}, u32[]{:S(2)}) async-start(f32[8,8,256]{2,1,0:T(8,128)} %broadcast_in_dim.299), calls=%async_computation.8 | async-start | bytes 131072 | tf_op jit(solution)/shard_map/all_to_all | solution.py:12
  156.4 6.8 %all-to-all-done.8 = f32[8,8,256]{2,1,0:T(8,128)S(1)} async-done(((f32[8,8,256]{2,1,0:T(8,128)}), f32[8,8,256]{2,1,0:T(8,128)S(1)}, u32[]{:S(2)}, u32[]{:S(2)}) %all-to-all-start.8) | async-done | bytes 65568 | tf_op jit(solution)/shard_map/all_to_all | solution.py:12
  (207 shorter events, 77.6 us)
Async XLA Ops:
  2.4 10.6 %collective-permute-start.2 = (bf16[112,256]{1,0:T(8,128)(2,1)S(1)}, bf16[112,256]{1,0:T(8,128)(2,1)S(1)}, u32[]{:S(2)}, u32[]{:S(2)}) collective-permute-start(bf16[112,256]{1,0:T(8,128)(2,1)S(1)} %get-tuple-element.721), channel_id=1, source_target_pairs={{0,32},{16,48},{32,0},{48,16},{1,33},{17,49},{33,1},{49,17},{2,34}... | collective-permute-start | bytes 172040 | tf_op jit(solution)/shard_map/while/body/eval_jaxpr/ppermute | solution.py:16
  8.8 7.3 %collective-permute-start.3 = (bf16[112,256]{1,0:T(8,128)(2,1)S(1)}, bf16[112,256]{1,0:T(8,128)(2,1)S(1)}, u32[]{:S(2)}, u32[]{:S(2)}) collective-permute-start(bf16[112,256]{1,0:T(8,128)(2,1)S(1)} %get-tuple-element.721), channel_id=1, source_target_pairs={{0,16},{16,32},{32,48},{48,0},{1,17},{17,33},{33,49},{49,1},{2,18}... | collective-permute-start | bytes 172040 | tf_op jit(solution)/shard_map/while/body/eval_jaxpr/ppermute | solution.py:16
  16.6 10.0 %collective-permute-start.5 = (bf16[4,112,256]{2,1,0:T(8,128)(2,1)S(1)}, bf16[4,112,256]{2,1,0:T(8,128)(2,1)S(1)}, u32[]{:S(2)}, u32[]{:S(2)}) collective-permute-start(bf16[4,112,256]{2,1,0:T(8,128)(2,1)S(1)} %bitcast_dynamic-update-slice_fusion.29), channel_id=1, source_target_pairs={{0,128},{64,192},{128,0},{192,64},{1,129},{65,193},{129,1},{193,65... | collective-permute-start | bytes 688136 | tf_op jit(solution)/shard_map/while/body/eval_jaxpr/ppermute | solution.py:16
  19.9 10.8 %collective-permute-start.6 = (bf16[4,112,256]{2,1,0:T(8,128)(2,1)S(1)}, bf16[4,112,256]{2,1,0:T(8,128)(2,1)S(1)}, u32[]{:S(2)}, u32[]{:S(2)}) collective-permute-start(bf16[4,112,256]{2,1,0:T(8,128)(2,1)S(1)} %bitcast_dynamic-update-slice_fusion.29), channel_id=1, source_target_pairs={{0,64},{64,128},{128,192},{192,0},{1,65},{65,129},{129,193},{193,1... | collective-permute-start | bytes 688136 | tf_op jit(solution)/shard_map/while/body/eval_jaxpr/ppermute | solution.py:16
  20.7 11.0 %collective-permute-start.7 = (bf16[4,112,256]{2,1,0:T(8,128)(2,1)S(1)}, bf16[4,112,256]{2,1,0:T(8,128)(2,1)S(1)}, u32[]{:S(2)}, u32[]{:S(2)}) collective-permute-start(bf16[4,112,256]{2,1,0:T(8,128)(2,1)S(1)} %bitcast_dynamic-update-slice_fusion.29), channel_id=1, source_target_pairs={{0,192},{64,0},{128,64},{192,128},{1,193},{65,1},{129,65},{193,129... | collective-permute-start | bytes 688136 | tf_op jit(solution)/shard_map/while/body/eval_jaxpr/ppermute | solution.py:16
  23.2 10.9 %collective-permute-start.9 = (bf16[4,112,256]{2,1,0:T(8,128)(2,1)S(1)}, bf16[4,112,256]{2,1,0:T(8,128)(2,1)S(1)}, u32[]{:S(2)}, u32[]{:S(2)}) collective-permute-start(bf16[4,112,256]{2,1,0:T(8,128)(2,1)S(1)} %collective-permute-done.8), channel_id=1, source_target_pairs={{0,64},{64,128},{128,192},{192,0},{1,65},{65,129},{129,193},{193,1... | collective-permute-start | bytes 688136 | tf_op jit(solution)/shard_map/while/body/eval_jaxpr/ppermute | solution.py:16
  23.5 10.6 %collective-permute-start.10 = (bf16[4,112,256]{2,1,0:T(8,128)(2,1)S(1)}, bf16[4,112,256]{2,1,0:T(8,128)(2,1)S(1)}, u32[]{:S(2)}, u32[]{:S(2)}) collective-permute-start(bf16[4,112,256]{2,1,0:T(8,128)(2,1)S(1)} %collective-permute-done.8), channel_id=1, source_target_pairs={{0,192},{64,0},{128,64},{192,128},{1,193},{65,1},{129,65},{193,129... | collective-permute-start | bytes 688136 | tf_op jit(solution)/shard_map/while/body/eval_jaxpr/ppermute | solution.py:16
  26.6 7.5 %collective-permute-start.11 = (bf16[4,112,256]{2,1,0:T(8,128)(2,1)S(1)}, bf16[4,112,256]{2,1,0:T(8,128)(2,1)S(1)}, u32[]{:S(2)}, u32[]{:S(2)}) collective-permute-start(bf16[4,112,256]{2,1,0:T(8,128)(2,1)S(1)} %collective-permute-done.5), channel_id=1, source_target_pairs={{0,8},{8,0},{1,9},{9,1},{2,10},{10,2},{3,11},{11,3},{4,12},{12,4},... | collective-permute-start | bytes 688136 | tf_op jit(solution)/shard_map/while/body/eval_jaxpr/ppermute | solution.py:35
  48.2 9.0 %collective-permute-start.2 = (bf16[112,256]{1,0:T(8,128)(2,1)S(1)}, bf16[112,256]{1,0:T(8,128)(2,1)S(1)}, u32[]{:S(2)}, u32[]{:S(2)}) collective-permute-start(bf16[112,256]{1,0:T(8,128)(2,1)S(1)} %get-tuple-element.721), channel_id=1, source_target_pairs={{0,32},{16,48},{32,0},{48,16},{1,33},{17,49},{33,1},{49,17},{2,34}... | collective-permute-start | bytes 172040 | tf_op jit(solution)/shard_map/while/body/eval_jaxpr/ppermute | solution.py:16
  60.4 10.1 %collective-permute-start.5 = (bf16[4,112,256]{2,1,0:T(8,128)(2,1)S(1)}, bf16[4,112,256]{2,1,0:T(8,128)(2,1)S(1)}, u32[]{:S(2)}, u32[]{:S(2)}) collective-permute-start(bf16[4,112,256]{2,1,0:T(8,128)(2,1)S(1)} %bitcast_dynamic-update-slice_fusion.29), channel_id=1, source_target_pairs={{0,128},{64,192},{128,0},{192,64},{1,129},{65,193},{129,1},{193,65... | collective-permute-start | bytes 688136 | tf_op jit(solution)/shard_map/while/body/eval_jaxpr/ppermute | solution.py:16
  62.9 11.2 %collective-permute-start.6 = (bf16[4,112,256]{2,1,0:T(8,128)(2,1)S(1)}, bf16[4,112,256]{2,1,0:T(8,128)(2,1)S(1)}, u32[]{:S(2)}, u32[]{:S(2)}) collective-permute-start(bf16[4,112,256]{2,1,0:T(8,128)(2,1)S(1)} %bitcast_dynamic-update-slice_fusion.29), channel_id=1, source_target_pairs={{0,64},{64,128},{128,192},{192,0},{1,65},{65,129},{129,193},{193,1... | collective-permute-start | bytes 688136 | tf_op jit(solution)/shard_map/while/body/eval_jaxpr/ppermute | solution.py:16
  64.4 11.2 %collective-permute-start.7 = (bf16[4,112,256]{2,1,0:T(8,128)(2,1)S(1)}, bf16[4,112,256]{2,1,0:T(8,128)(2,1)S(1)}, u32[]{:S(2)}, u32[]{:S(2)}) collective-permute-start(bf16[4,112,256]{2,1,0:T(8,128)(2,1)S(1)} %bitcast_dynamic-update-slice_fusion.29), channel_id=1, source_target_pairs={{0,192},{64,0},{128,64},{192,128},{1,193},{65,1},{129,65},{193,129... | collective-permute-start | bytes 688136 | tf_op jit(solution)/shard_map/while/body/eval_jaxpr/ppermute | solution.py:16
  66.4 11.7 %collective-permute-start.9 = (bf16[4,112,256]{2,1,0:T(8,128)(2,1)S(1)}, bf16[4,112,256]{2,1,0:T(8,128)(2,1)S(1)}, u32[]{:S(2)}, u32[]{:S(2)}) collective-permute-start(bf16[4,112,256]{2,1,0:T(8,128)(2,1)S(1)} %collective-permute-done.8), channel_id=1, source_target_pairs={{0,64},{64,128},{128,192},{192,0},{1,65},{65,129},{129,193},{193,1... | collective-permute-start | bytes 688136 | tf_op jit(solution)/shard_map/while/body/eval_jaxpr/ppermute | solution.py:16
  68.0 10.4 %collective-permute-start.10 = (bf16[4,112,256]{2,1,0:T(8,128)(2,1)S(1)}, bf16[4,112,256]{2,1,0:T(8,128)(2,1)S(1)}, u32[]{:S(2)}, u32[]{:S(2)}) collective-permute-start(bf16[4,112,256]{2,1,0:T(8,128)(2,1)S(1)} %collective-permute-done.8), channel_id=1, source_target_pairs={{0,192},{64,0},{128,64},{192,128},{1,193},{65,1},{129,65},{193,129... | collective-permute-start | bytes 688136 | tf_op jit(solution)/shard_map/while/body/eval_jaxpr/ppermute | solution.py:16
  70.6 7.9 %collective-permute-start.11 = (bf16[4,112,256]{2,1,0:T(8,128)(2,1)S(1)}, bf16[4,112,256]{2,1,0:T(8,128)(2,1)S(1)}, u32[]{:S(2)}, u32[]{:S(2)}) collective-permute-start(bf16[4,112,256]{2,1,0:T(8,128)(2,1)S(1)} %collective-permute-done.5), channel_id=1, source_target_pairs={{0,8},{8,0},{1,9},{9,1},{2,10},{10,2},{3,11},{11,3},{4,12},{12,4},... | collective-permute-start | bytes 688136 | tf_op jit(solution)/shard_map/while/body/eval_jaxpr/ppermute | solution.py:35
  92.5 8.2 %collective-permute-start.2 = (bf16[112,256]{1,0:T(8,128)(2,1)S(1)}, bf16[112,256]{1,0:T(8,128)(2,1)S(1)}, u32[]{:S(2)}, u32[]{:S(2)}) collective-permute-start(bf16[112,256]{1,0:T(8,128)(2,1)S(1)} %get-tuple-element.721), channel_id=1, source_target_pairs={{0,32},{16,48},{32,0},{48,16},{1,33},{17,49},{33,1},{49,17},{2,34}... | collective-permute-start | bytes 172040 | tf_op jit(solution)/shard_map/while/body/eval_jaxpr/ppermute | solution.py:16
  102.9 7.2 %collective-permute-start.8 = (bf16[4,112,256]{2,1,0:T(8,128)(2,1)S(1)}, bf16[4,112,256]{2,1,0:T(8,128)(2,1)S(1)}, u32[]{:S(2)}, u32[]{:S(2)}) collective-permute-start(bf16[4,112,256]{2,1,0:T(8,128)(2,1)S(1)} %bitcast_dynamic-update-slice_fusion.29), channel_id=1, source_target_pairs={{0,8},{8,0},{1,9},{9,1},{2,10},{10,2},{3,11},{11,3},{4,12},{12,4},... | collective-permute-start | bytes 688136 | tf_op jit(solution)/shard_map/while/body/eval_jaxpr/ppermute | solution.py:33
  104.3 10.0 %collective-permute-start.5 = (bf16[4,112,256]{2,1,0:T(8,128)(2,1)S(1)}, bf16[4,112,256]{2,1,0:T(8,128)(2,1)S(1)}, u32[]{:S(2)}, u32[]{:S(2)}) collective-permute-start(bf16[4,112,256]{2,1,0:T(8,128)(2,1)S(1)} %bitcast_dynamic-update-slice_fusion.29), channel_id=1, source_target_pairs={{0,128},{64,192},{128,0},{192,64},{1,129},{65,193},{129,1},{193,65... | collective-permute-start | bytes 688136 | tf_op jit(solution)/shard_map/while/body/eval_jaxpr/ppermute | solution.py:16
  106.8 11.2 %collective-permute-start.6 = (bf16[4,112,256]{2,1,0:T(8,128)(2,1)S(1)}, bf16[4,112,256]{2,1,0:T(8,128)(2,1)S(1)}, u32[]{:S(2)}, u32[]{:S(2)}) collective-permute-start(bf16[4,112,256]{2,1,0:T(8,128)(2,1)S(1)} %bitcast_dynamic-update-slice_fusion.29), channel_id=1, source_target_pairs={{0,64},{64,128},{128,192},{192,0},{1,65},{65,129},{129,193},{193,1... | collective-permute-start | bytes 688136 | tf_op jit(solution)/shard_map/while/body/eval_jaxpr/ppermute | solution.py:16
  108.1 10.8 %collective-permute-start.7 = (bf16[4,112,256]{2,1,0:T(8,128)(2,1)S(1)}, bf16[4,112,256]{2,1,0:T(8,128)(2,1)S(1)}, u32[]{:S(2)}, u32[]{:S(2)}) collective-permute-start(bf16[4,112,256]{2,1,0:T(8,128)(2,1)S(1)} %bitcast_dynamic-update-slice_fusion.29), channel_id=1, source_target_pairs={{0,192},{64,0},{128,64},{192,128},{1,193},{65,1},{129,65},{193,129... | collective-permute-start | bytes 688136 | tf_op jit(solution)/shard_map/while/body/eval_jaxpr/ppermute | solution.py:16
  110.1 11.3 %collective-permute-start.9 = (bf16[4,112,256]{2,1,0:T(8,128)(2,1)S(1)}, bf16[4,112,256]{2,1,0:T(8,128)(2,1)S(1)}, u32[]{:S(2)}, u32[]{:S(2)}) collective-permute-start(bf16[4,112,256]{2,1,0:T(8,128)(2,1)S(1)} %collective-permute-done.8), channel_id=1, source_target_pairs={{0,64},{64,128},{128,192},{192,0},{1,65},{65,129},{129,193},{193,1... | collective-permute-start | bytes 688136 | tf_op jit(solution)/shard_map/while/body/eval_jaxpr/ppermute | solution.py:16
  110.4 11.0 %collective-permute-start.10 = (bf16[4,112,256]{2,1,0:T(8,128)(2,1)S(1)}, bf16[4,112,256]{2,1,0:T(8,128)(2,1)S(1)}, u32[]{:S(2)}, u32[]{:S(2)}) collective-permute-start(bf16[4,112,256]{2,1,0:T(8,128)(2,1)S(1)} %collective-permute-done.8), channel_id=1, source_target_pairs={{0,192},{64,0},{128,64},{192,128},{1,193},{65,1},{129,65},{193,129... | collective-permute-start | bytes 688136 | tf_op jit(solution)/shard_map/while/body/eval_jaxpr/ppermute | solution.py:16
  126.0 7.6 %collective-permute-start.16 = (f32[104,256]{1,0:T(8,128)S(1)}, f32[104,256]{1,0:T(8,128)S(1)}, u32[]{:S(2)}, u32[]{:S(2)}) collective-permute-start(f32[104,256]{1,0:T(8,128)S(1)} %get-tuple-element.689), channel_id=1, source_target_pairs={{0,6},{2,0},{4,2},{6,4},{1,7},{3,1},{5,3},{7,5},{8,14},{10,8},{12,... | collective-permute-start | bytes 319496 | tf_op jit(solution)/shard_map/while/body/eval_jaxpr/ppermute | solution.py:16
  151.0 12.2 %all-to-all-start.8 = ((f32[8,8,256]{2,1,0:T(8,128)}), f32[8,8,256]{2,1,0:T(8,128)S(1)}, u32[]{:S(2)}, u32[]{:S(2)}) async-start(f32[8,8,256]{2,1,0:T(8,128)} %broadcast_in_dim.299), calls=%async_computation.8 | async-start | bytes 131072 | tf_op jit(solution)/shard_map/all_to_all | solution.py:12
  (34 other events, 182.7 us)
